TPU v7x, 512 devices: a whole 4x8x8 slice. The times are simulated.
512 devices in a mesh: los: 16 (over z_hi, y), sky: 32 (over x, z_lo, core).
Axes of the slice: x: 4, y: 8, z: 8 (z_hi: 2, z_lo: 4; z = z_hi * 4 + z_lo), core: 2. Of those that a mesh axis runs over, the one named last changes fastest.
Arguments:
- state: float32 [12, 524288], P(None, ('los', 'sky')), may hold values from -6 to 6
- deflection: bfloat16 [16, 2, 64, 8192], P('los', None, None, 'sky'), may hold values from -6 to 6
- shear: bfloat16 [16, 2, 96, 8192], P('los', None, None, 'sky'), may hold values from -3 to 3
- routes: int32 [4, 2, 524288, 1], P(None, None, ('los', 'sky')), may hold values from 0 to 31; in each aligned block of 1024 rows (0 to 1023, 1024 to 2047, ..., all dimensions but the last counted through in order) at most 64 rows name the same one
- patches: int32 [4, 2, 524288], P(None, None, ('los', 'sky')), may hold values from 0 to 255
Outputs:
- traced: float32 [12, 524288], P(None, ('los', 'sky'))
Inputs may be any that keep to these rules, and one draw needn't show every extreme that they name: `routes`: in each hop and plane, one device's 1024 slots name one tile at most 64 times, and exactly 64 times in some.
All inputs are finite; a program needn't handle non-finite values.
Results may differ from a plain program's by a relative error of at most 0.0003.
Values sent between devices are 32-bit elements; how exact they have to be, the bound alone decides.
No kernel may reach another device: no remote copies, remote signals or barrier semaphores. Data moves between devices by JAX's collectives and lax.ppermute only.
A program may use at most 64 MiB of HBM per device.

v0:
```python
import math

import jax
import jax.numpy as jnp
from jax import lax
from jax.sharding import PartitionSpec as P


def shifted(block, axis, distance):
    devices = range(lax.axis_size(axis))
    route = [((i - distance) % len(devices), i) for i in devices]
    return lax.ppermute(block, axis, route)


def weights(pos_x, pos_y):
    across = jnp.arange(4).astype(pos_x.dtype)
    along = jnp.arange(8).astype(pos_x.dtype)
    kern_x = (1.0 + jnp.cos(2.0 * math.pi * (pos_x[None, :] - across[:, None]) / 4.0)) / 4.0
    kern_y = (1.0 + jnp.cos(2.0 * math.pi * (pos_y[None, :] - along[:, None]) / 8.0)) / 8.0
    return (kern_x[:, None, :] * kern_y[None, :, :]).reshape(32, -1)


def interpolate(raw, pos_x, pos_y):
    table = weights(pos_x, pos_y)
    return jnp.sum(raw.reshape(5, 32, -1) * table[None], axis=1)


def advance(current, values):
    pos_x, pos_y, ang_x, ang_y, a11, a12, a21, a22, b11, b12, b21, b22 = [
        current[k] for k in range(12)
    ]
    alpha_x, alpha_y, psi11, psi12, psi22 = [values[k] for k in range(5)]
    ang_x = ang_x - alpha_x
    ang_y = ang_y - alpha_y
    b11 = b11 - (psi11 * a11 + psi12 * a21)
    b12 = b12 - (psi11 * a12 + psi12 * a22)
    b21 = b21 - (psi12 * a11 + psi22 * a21)
    b22 = b22 - (psi12 * a12 + psi22 * a22)
    pos_x = pos_x + 0.5 * ang_x
    pos_y = pos_y + 0.5 * ang_y
    a11 = a11 + 0.5 * b11
    a12 = a12 + 0.5 * b12
    a21 = a21 + 0.5 * b21
    a22 = a22 + 0.5 * b22
    return jnp.stack([pos_x, pos_y, ang_x, ang_y, a11, a12, a21, a22, b11, b12, b21, b22])


def lookup(fields, pos_x, pos_y, patch):
    count = fields.shape[1]
    onehot = (patch[None, :] == jnp.arange(count, dtype=jnp.int32)[:, None]).astype(jnp.bfloat16)
    raw = jnp.dot(fields, onehot, preferred_element_type=jnp.float32)
    return interpolate(raw, pos_x, pos_y)


def arrange(dest, tiles, capacity):
    ray_count = dest.shape[0]
    member = (dest[None, :] == jnp.arange(tiles, dtype=jnp.int32)[:, None]).astype(jnp.int32)
    running = jnp.cumsum(member, axis=1)
    rank = jnp.sum(member * (running - 1), axis=0)
    slot = dest * capacity + rank
    source = jnp.full((tiles * capacity,), ray_count, jnp.int32)
    source = source.at[slot].set(jnp.arange(ray_count, dtype=jnp.int32))
    filled = source < ray_count
    source = jnp.minimum(source, ray_count - 1)
    return (slot, source, filled)


def collect(values, source, filled, tiles, capacity):
    taken = jnp.take(values, source, axis=1)
    taken = jnp.where(filled[None, :], taken, jnp.zeros_like(taken))
    return taken.reshape(values.shape[0], tiles, capacity)


def body(state, deflection, shear, routes, patches):
    ray_count = state.shape[1]
    tiles = lax.axis_size("sky")
    capacity = 2 * ray_count // tiles
    for hop in range(routes.shape[0]):
        for plane in range(2):
            fields = jnp.concatenate([deflection[0, plane], shear[0, plane]], axis=0)
            slot, source, filled = arrange(routes[hop, plane, :, 0], tiles, capacity)
            sent_patch = collect(patches[hop, plane][None, :], source, filled, tiles, capacity)
            sent = collect(state, source, filled, tiles, capacity)

            def visit_whole(parts, fields=fields):
                rays, patch = parts
                flat = rays.reshape(12, -1)
                values = lookup(fields, flat[0], flat[1], patch.reshape(-1))
                moved = advance(flat, values).reshape(rays.shape)
                return lax.all_to_all(moved, "sky", split_axis=1, concat_axis=1, tiled=True)

            back = visit_whole(
                (
                    lax.all_to_all(sent, "sky", split_axis=1, concat_axis=1, tiled=True),
                    lax.all_to_all(sent_patch, "sky", split_axis=1, concat_axis=1, tiled=True),
                )
            )
            state = jnp.take(back.reshape(12, tiles * capacity), slot, axis=1)
        state = shifted(state, "los", 1)
    return state


def solution(mesh):
    placed = (
        P(None, ("los", "sky")),
        P("los", None, None, "sky"),
        P("los", None, None, "sky"),
        P(None, None, ("los", "sky"), None),
        P(None, None, ("los", "sky")),
    )
    return jax.shard_map(
        body, mesh=mesh, in_specs=placed, out_specs=P(None, ("los", "sky")), check_vma=False
    )
```

profile of v0, /device:TPU:56, one launch (start us, length us, event | category | flops | bytes accessed | tf_op | source)
XLA Modules:
  0.0 740.9 jit_solution(1577738789076412414)
XLA Ops:
  0.9 9.0 %reduce-window.56 = s32[32,8,128]{2,1,0:T(8,128)S(1)} reduce-window(s32[32,8,128]{2,1,0:T(8,128)S(1)} %fusion.22, s32[]{:T(128)} %constant.123.clone.1), window={size=1x1x128 pad=0_0x0_0x127_0}, to_apply=%region_4.5 | reduce-window | flops 4161536 | bytes 262148 | tf_op jit(solution)/shard_map/reduce-window.2
  10.4 9.0 %reduce-window.60 = s32[32,8,128]{2,1,0:T(8,128)S(1)} reduce-window(s32[32,8,128]{2,1,0:T(8,128)S(1)} %fusion.21, s32[]{:T(128)} %constant.123.clone.1), window={size=1x1x128 pad=0_0x0_0x127_0}, to_apply=%region_8.9 | reduce-window | flops 4161536 | bytes 262148 | tf_op jit(solution)/shard_map/reduce-window.4
  19.9 9.0 %reduce-window.64 = s32[32,8,128]{2,1,0:T(8,128)S(1)} reduce-window(s32[32,8,128]{2,1,0:T(8,128)S(1)} %fusion.20, s32[]{:T(128)} %constant.123.clone.1), window={size=1x1x128 pad=0_0x0_0x127_0}, to_apply=%region_12.13 | reduce-window | flops 4161536 | bytes 262148 | tf_op jit(solution)/shard_map/reduce-window.6
  29.3 9.0 %reduce-window.66 = s32[32,8,128]{2,1,0:T(8,128)S(1)} reduce-window(s32[32,8,128]{2,1,0:T(8,128)S(1)} %fusion.19, s32[]{:T(128)} %constant.123.clone.1), window={size=1x1x128 pad=0_0x0_0x127_0}, to_apply=%region_16.17 | reduce-window | flops 4161536 | bytes 262148 | tf_op jit(solution)/shard_map/reduce-window.8
  38.8 9.0 %reduce-window.70 = s32[32,8,128]{2,1,0:T(8,128)S(1)} reduce-window(s32[32,8,128]{2,1,0:T(8,128)S(1)} %fusion.18, s32[]{:T(128)} %constant.123.clone.1), window={size=1x1x128 pad=0_0x0_0x127_0}, to_apply=%region_20.21 | reduce-window | flops 4161536 | bytes 262148 | tf_op jit(solution)/shard_map/reduce-window.10
  48.3 9.0 %reduce-window.74 = s32[32,8,128]{2,1,0:T(8,128)S(1)} reduce-window(s32[32,8,128]{2,1,0:T(8,128)S(1)} %fusion.17, s32[]{:T(128)} %constant.123.clone.1), window={size=1x1x128 pad=0_0x0_0x127_0}, to_apply=%region_24.25 | reduce-window | flops 4161536 | bytes 262148 | tf_op jit(solution)/shard_map/reduce-window.12
  57.8 9.0 %reduce-window.54 = s32[32,8,128]{2,1,0:T(8,128)S(1)} reduce-window(s32[32,8,128]{2,1,0:T(8,128)S(1)} %fusion.23, s32[]{:T(128)} %constant.123.clone.1), window={size=1x1x128 pad=0_0x0_0x127_0}, to_apply=%region_0.0 | reduce-window | flops 4161536 | bytes 262148 | tf_op jit(solution)/shard_map/reduce-window
  67.3 9.0 %reduce-window.76 = s32[32,8,128]{2,1,0:T(8,128)S(1)} reduce-window(s32[32,8,128]{2,1,0:T(8,128)S(1)} %fusion.16, s32[]{:T(128)} %constant.123.clone.1), window={size=1x1x128 pad=0_0x0_0x127_0}, to_apply=%region_28.29 | reduce-window | flops 4161536 | bytes 262148 | tf_op jit(solution)/shard_map/reduce-window.14
  81.3 8.6 %gather_fusion.1 = s32[2048]{0:T(1024)S(1)} fusion(s32[1024]{0:T(1024)S(1)} %bitcast.327, s32[2048]{0:T(1024)S(1)} %fusion.32), kind=kCustom, calls=%fused_computation.1.clone | custom fusion | bytes 24576 | tf_op jit(solution)/shard_map/jit(_take)/gather | solution.py:69
  90.7 10.1 %all-to-all-start.1 = ((s32[1,32,64]{2,0,1:T(1,128)}), s32[1,32,64]{2,0,1:T(1,128)S(1)}, u32[]{:S(2)}, u32[]{:S(2)}) async-start(s32[1,32,64]{2,0,1:T(1,128)} %reshape.1815), calls=%async_computation.1 | async-start | bytes 32768 | tf_op jit(solution)/shard_map/all_to_all | solution.py:95
  137.3 8.6 %gather_fusion.4 = s32[2048]{0:T(1024)S(1)} fusion(s32[1024]{0:T(1024)S(1)} %bitcast.326, s32[2048]{0:T(1024)S(1)} %fusion.33), kind=kCustom, calls=%fused_computation.10.clone | custom fusion | bytes 24576 | tf_op jit(solution)/shard_map/jit(_take)/gather | solution.py:69
  145.9 8.6 %gather_fusion.7 = s32[2048]{0:T(1024)S(1)} fusion(s32[1024]{0:T(1024)S(1)} %bitcast.325, s32[2048]{0:T(1024)S(1)} %fusion.34), kind=kCustom, calls=%fused_computation.11.clone | custom fusion | bytes 24576 | tf_op jit(solution)/shard_map/jit(_take)/gather | solution.py:69
  154.5 8.6 %gather_fusion.10 = s32[2048]{0:T(1024)S(1)} fusion(s32[1024]{0:T(1024)S(1)} %bitcast.324, s32[2048]{0:T(1024)S(1)} %fusion.35), kind=kCustom, calls=%fused_computation.12.clone | custom fusion | bytes 24576 | tf_op jit(solution)/shard_map/jit(_take)/gather | solution.py:69
  163.1 8.6 %gather_fusion.13 = s32[2048]{0:T(1024)S(1)} fusion(s32[1024]{0:T(1024)S(1)} %bitcast.323, s32[2048]{0:T(1024)S(1)} %fusion.36), kind=kCustom, calls=%fused_computation.13.clone | custom fusion | bytes 24576 | tf_op jit(solution)/shard_map/jit(_take)/gather | solution.py:69
  171.7 8.6 %gather_fusion.16 = s32[2048]{0:T(1024)S(1)} fusion(s32[1024]{0:T(1024)S(1)} %bitcast.322, s32[2048]{0:T(1024)S(1)} %fusion.37), kind=kCustom, calls=%fused_computation.14.clone | custom fusion | bytes 24576 | tf_op jit(solution)/shard_map/jit(_take)/gather | solution.py:69
  180.4 8.6 %gather_fusion.19 = s32[2048]{0:T(1024)S(1)} fusion(s32[1024]{0:T(1024)S(1)} %bitcast.321, s32[2048]{0:T(1024)S(1)} %fusion.38), kind=kCustom, calls=%fused_computation.15.clone | custom fusion | bytes 24576 | tf_op jit(solution)/shard_map/jit(_take)/gather | solution.py:69
  189.0 8.6 %gather_fusion.22 = s32[2048]{0:T(1024)S(1)} fusion(s32[1024]{0:T(1024)S(1)} %bitcast.320, s32[2048]{0:T(1024)S(1)} %fusion.39), kind=kCustom, calls=%fused_computation.16.clone | custom fusion | bytes 24576 | tf_op jit(solution)/shard_map/jit(_take)/gather | solution.py:69
  282.5 8.4 %all-to-all-done.5 = f32[32,1,768]{2,1,0:T(1,128)S(1)} async-done(((f32[32,1,768]{2,1,0:T(1,128)}), f32[32,1,768]{2,1,0:T(1,128)S(1)}, u32[]{:S(2)}, u32[]{:S(2)}) %all-to-all-start.5) | async-done | bytes 98336 | tf_op jit(solution)/shard_map/all_to_all | solution.py:90
  308.6 17.6 %collective-permute-done = f32[12,1024]{0,1:T(8,128)S(1)} collective-permute-done((f32[12,1024]{0,1:T(8,128)S(1)}, f32[12,1024]{0,1:T(8,128)S(1)}, u32[]{:S(2)}, u32[]{:S(2)}) %collective-permute-start) | collective-permute-done | bytes 49184 | tf_op jit(solution)/shard_map/ppermute | solution.py:12
  333.6 8.8 %all-to-all-start.6 = ((f32[32,1,768]{2,1,0:T(1,128)}), f32[32,1,768]{2,1,0:T(1,128)S(1)}, u32[]{:S(2)}, u32[]{:S(2)}) async-start(f32[32,1,768]{2,1,0:T(1,128)} %reshape.3402), calls=%async_computation.6 | async-start | bytes 196608 | tf_op jit(solution)/shard_map/all_to_all | solution.py:94
  343.0 7.9 %all-to-all-done.6 = f32[32,1,768]{2,1,0:T(1,128)S(1)} async-done(((f32[32,1,768]{2,1,0:T(1,128)}), f32[32,1,768]{2,1,0:T(1,128)S(1)}, u32[]{:S(2)}, u32[]{:S(2)}) %all-to-all-start.6) | async-done | bytes 98336 | tf_op jit(solution)/shard_map/all_to_all | solution.py:94
  415.6 8.4 %all-to-all-done.11 = f32[32,1,768]{2,1,0:T(1,128)S(1)} async-done(((f32[32,1,768]{2,1,0:T(1,128)}), f32[32,1,768]{2,1,0:T(1,128)S(1)}, u32[]{:S(2)}, u32[]{:S(2)}) %all-to-all-start.11) | async-done | bytes 98336 | tf_op jit(solution)/shard_map/all_to_all | solution.py:90
  432.2 12.6 %collective-permute-start.1 = (f32[12,1024]{0,1:T(8,128)S(1)}, f32[12,1024]{0,1:T(8,128)S(1)}, u32[]{:S(2)}, u32[]{:S(2)}) collective-permute-start(f32[12,1024]{0,1:T(8,128)S(1)} %select_bitcast_fusion.4), channel_id=1, source_target_pairs={{480,0},{0,32},{32,64},{64,96},{96,128},{128,160},{160,192},{192,2... | collective-permute-start | bytes 147464 | tf_op jit(solution)/shard_map/ppermute | solution.py:12
  447.0 17.7 %collective-permute-done.1 = f32[12,1024]{0,1:T(8,128)S(1)} collective-permute-done((f32[12,1024]{0,1:T(8,128)S(1)}, f32[12,1024]{0,1:T(8,128)S(1)}, u32[]{:S(2)}, u32[]{:S(2)}) %collective-permute-start.1) | collective-permute-done | bytes 49184 | tf_op jit(solution)/shard_map/ppermute | solution.py:12
  472.1 9.0 %all-to-all-start.12 = ((f32[32,1,768]{2,1,0:T(1,128)}), f32[32,1,768]{2,1,0:T(1,128)S(1)}, u32[]{:S(2)}, u32[]{:S(2)}) async-start(f32[32,1,768]{2,1,0:T(1,128)} %reshape.3410), calls=%async_computation.12 | async-start | bytes 196608 | tf_op jit(solution)/shard_map/all_to_all | solution.py:94
  554.4 8.4 %all-to-all-done.17 = f32[32,1,768]{2,1,0:T(1,128)S(1)} async-done(((f32[32,1,768]{2,1,0:T(1,128)}), f32[32,1,768]{2,1,0:T(1,128)S(1)}, u32[]{:S(2)}, u32[]{:S(2)}) %all-to-all-start.17) | async-done | bytes 98336 | tf_op jit(solution)/shard_map/all_to_all | solution.py:90
  571.0 12.6 %collective-permute-start.2 = (f32[12,1024]{0,1:T(8,128)S(1)}, f32[12,1024]{0,1:T(8,128)S(1)}, u32[]{:S(2)}, u32[]{:S(2)}) collective-permute-start(f32[12,1024]{0,1:T(8,128)S(1)} %select_bitcast_fusion.2), channel_id=1, source_target_pairs={{480,0},{0,32},{32,64},{64,96},{96,128},{128,160},{160,192},{192,2... | collective-permute-start | bytes 147464 | tf_op jit(solution)/shard_map/ppermute | solution.py:12
  585.0 18.6 %collective-permute-done.2 = f32[12,1024]{0,1:T(8,128)S(1)} collective-permute-done((f32[12,1024]{0,1:T(8,128)S(1)}, f32[12,1024]{0,1:T(8,128)S(1)}, u32[]{:S(2)}, u32[]{:S(2)}) %collective-permute-start.2) | collective-permute-done | bytes 49184 | tf_op jit(solution)/shard_map/ppermute | solution.py:12
  611.0 9.3 %all-to-all-start.18 = ((f32[32,1,768]{2,1,0:T(1,128)}), f32[32,1,768]{2,1,0:T(1,128)S(1)}, u32[]{:S(2)}, u32[]{:S(2)}) async-start(f32[32,1,768]{2,1,0:T(1,128)} %reshape.3418), calls=%async_computation.18 | async-start | bytes 196608 | tf_op jit(solution)/shard_map/all_to_all | solution.py:94
  693.3 8.4 %all-to-all-done.23 = f32[32,1,768]{2,1,0:T(1,128)S(1)} async-done(((f32[32,1,768]{2,1,0:T(1,128)}), f32[32,1,768]{2,1,0:T(1,128)S(1)}, u32[]{:S(2)}, u32[]{:S(2)}) %all-to-all-start.23) | async-done | bytes 98336 | tf_op jit(solution)/shard_map/all_to_all | solution.py:90
  706.1 12.9 %collective-permute-start.3 = (f32[12,1024]{0,1:T(8,128)S(1)}, f32[12,1024]{0,1:T(8,128)S(1)}, u32[]{:S(2)}, u32[]{:S(2)}) collective-permute-start(f32[12,1024]{0,1:T(8,128)S(1)} %select_bitcast_fusion), channel_id=1, source_target_pairs={{480,0},{0,32},{32,64},{64,96},{96,128},{128,160},{160,192},{192,2... | collective-permute-start | bytes 147464 | tf_op jit(solution)/shard_map/ppermute | solution.py:12
  719.0 20.7 %collective-permute-done.3 = f32[12,1024]{0,1:T(8,128)S(1)} collective-permute-done((f32[12,1024]{0,1:T(8,128)S(1)}, f32[12,1024]{0,1:T(8,128)S(1)}, u32[]{:S(2)}, u32[]{:S(2)}) %collective-permute-start.3) | collective-permute-done | bytes 49184 | tf_op jit(solution)/shard_map/ppermute | solution.py:12
  (701 shorter events, 405.1 us)
Async XLA Ops:
  57.4 23.9 %copy-start.4 = (s32[4,2,1024]{2,1,0:T(2,128)S(1)}, s32[4,2,1024]{2,1,0:T(2,128)}, u32[]{:S(2)}) copy-start(s32[4,2,1024]{2,1,0:T(2,128)} %param.15) | copy-start | bytes 98308
  81.3 50.3 %copy-start.2 = (f32[12,1024]{1,0:T(8,128)S(1)}, f32[12,1024]{1,0:T(8,128)}, u32[]{:S(2)}) copy-start(f32[12,1024]{1,0:T(8,128)} %param.11) | copy-start | bytes 147460
  89.9 47.4 %copy-start.1 = (bf16[1,2,96,256]{3,2,1,0:T(8,128)(2,1)S(1)}, bf16[1,2,96,256]{3,2,1,0:T(8,128)(2,1)}, u32[]{:S(2)}) copy-start(bf16[1,2,96,256]{3,2,1,0:T(8,128)(2,1)} %param.13) | copy-start | bytes 294916
  89.9 47.4 %copy-start.3 = (bf16[1,2,64,256]{3,2,1,0:T(8,128)(2,1)S(1)}, bf16[1,2,64,256]{3,2,1,0:T(8,128)(2,1)}, u32[]{:S(2)}) copy-start(bf16[1,2,64,256]{3,2,1,0:T(8,128)(2,1)} %param.12) | copy-start | bytes 196612
  90.7 110.3 %all-to-all-start.1 = ((s32[1,32,64]{2,0,1:T(1,128)}), s32[1,32,64]{2,0,1:T(1,128)S(1)}, u32[]{:S(2)}, u32[]{:S(2)}) async-start(s32[1,32,64]{2,0,1:T(1,128)} %reshape.1815), calls=%async_computation.1 | async-start | bytes 32768 | tf_op jit(solution)/shard_map/all_to_all | solution.py:95
  201.0 16.1 %all-to-all-start = ((f32[32,1,768]{2,1,0:T(1,128)}), f32[32,1,768]{2,1,0:T(1,128)S(1)}, u32[]{:S(2)}, u32[]{:S(2)}) async-start(f32[32,1,768]{2,1,0:T(1,128)} %reshape.3394), calls=%async_computation | async-start | bytes 196608 | tf_op jit(solution)/shard_map/all_to_all | solution.py:94
  217.1 12.6 %all-to-all-start.4 = ((s32[1,32,64]{2,0,1:T(1,128)}), s32[1,32,64]{2,0,1:T(1,128)S(1)}, u32[]{:S(2)}, u32[]{:S(2)}) async-start(s32[1,32,64]{2,0,1:T(1,128)} %reshape.1819), calls=%async_computation.4 | async-start | bytes 32768 | tf_op jit(solution)/shard_map/all_to_all | solution.py:95
  229.7 16.1 %all-to-all-start.2 = ((f32[32,1,768]{2,1,0:T(1,128)}), f32[32,1,768]{2,1,0:T(1,128)S(1)}, u32[]{:S(2)}, u32[]{:S(2)}) async-start(f32[32,1,768]{2,1,0:T(1,128)} %reshape.3396), calls=%async_computation.2 | async-start | bytes 196608 | tf_op jit(solution)/shard_map/all_to_all | solution.py:90
  257.6 12.7 %all-to-all-start.3 = ((f32[32,1,768]{2,1,0:T(1,128)}), f32[32,1,768]{2,1,0:T(1,128)S(1)}, u32[]{:S(2)}, u32[]{:S(2)}) async-start(f32[32,1,768]{2,1,0:T(1,128)} %reshape.3398), calls=%async_computation.3 | async-start | bytes 196608 | tf_op jit(solution)/shard_map/all_to_all | solution.py:94
  278.6 12.3 %all-to-all-start.5 = ((f32[32,1,768]{2,1,0:T(1,128)}), f32[32,1,768]{2,1,0:T(1,128)S(1)}, u32[]{:S(2)}, u32[]{:S(2)}) async-start(f32[32,1,768]{2,1,0:T(1,128)} %reshape.3400), calls=%async_computation.5 | async-start | bytes 196608 | tf_op jit(solution)/shard_map/all_to_all | solution.py:90
  290.9 17.0 %all-to-all-start.7 = ((s32[1,32,64]{2,0,1:T(1,128)}), s32[1,32,64]{2,0,1:T(1,128)S(1)}, u32[]{:S(2)}, u32[]{:S(2)}) async-start(s32[1,32,64]{2,0,1:T(1,128)} %reshape.1823), calls=%async_computation.7 | async-start | bytes 32768 | tf_op jit(solution)/shard_map/all_to_all | solution.py:95
  299.0 27.2 %collective-permute-start = (f32[12,1024]{0,1:T(8,128)S(1)}, f32[12,1024]{0,1:T(8,128)S(1)}, u32[]{:S(2)}, u32[]{:S(2)}) collective-permute-start(f32[12,1024]{0,1:T(8,128)S(1)} %select_bitcast_fusion.6), channel_id=1, source_target_pairs={{480,0},{0,32},{32,64},{64,96},{96,128},{128,160},{160,192},{192,2... | collective-permute-start | bytes 147464 | tf_op jit(solution)/shard_map/ppermute | solution.py:12
  333.6 17.3 %all-to-all-start.6 = ((f32[32,1,768]{2,1,0:T(1,128)}), f32[32,1,768]{2,1,0:T(1,128)S(1)}, u32[]{:S(2)}, u32[]{:S(2)}) async-start(f32[32,1,768]{2,1,0:T(1,128)} %reshape.3402), calls=%async_computation.6 | async-start | bytes 196608 | tf_op jit(solution)/shard_map/all_to_all | solution.py:94
  350.9 12.2 %all-to-all-start.10 = ((s32[1,32,64]{2,0,1:T(1,128)}), s32[1,32,64]{2,0,1:T(1,128)S(1)}, u32[]{:S(2)}, u32[]{:S(2)}) async-start(s32[1,32,64]{2,0,1:T(1,128)} %reshape.1827), calls=%async_computation.10 | async-start | bytes 32768 | tf_op jit(solution)/shard_map/all_to_all | solution.py:95
  363.1 16.3 %all-to-all-start.8 = ((f32[32,1,768]{2,1,0:T(1,128)}), f32[32,1,768]{2,1,0:T(1,128)S(1)}, u32[]{:S(2)}, u32[]{:S(2)}) async-start(f32[32,1,768]{2,1,0:T(1,128)} %reshape.3404), calls=%async_computation.8 | async-start | bytes 196608 | tf_op jit(solution)/shard_map/all_to_all | solution.py:90
  391.1 12.3 %all-to-all-start.9 = ((f32[32,1,768]{2,1,0:T(1,128)}), f32[32,1,768]{2,1,0:T(1,128)S(1)}, u32[]{:S(2)}, u32[]{:S(2)}) async-start(f32[32,1,768]{2,1,0:T(1,128)} %reshape.3406), calls=%async_computation.9 | async-start | bytes 196608 | tf_op jit(solution)/shard_map/all_to_all | solution.py:94
  411.7 12.3 %all-to-all-start.11 = ((f32[32,1,768]{2,1,0:T(1,128)}), f32[32,1,768]{2,1,0:T(1,128)S(1)}, u32[]{:S(2)}, u32[]{:S(2)}) async-start(f32[32,1,768]{2,1,0:T(1,128)} %reshape.3408), calls=%async_computation.11 | async-start | bytes 196608 | tf_op jit(solution)/shard_map/all_to_all | solution.py:90
  424.0 22.2 %all-to-all-start.13 = ((s32[1,32,64]{2,0,1:T(1,128)}), s32[1,32,64]{2,0,1:T(1,128)S(1)}, u32[]{:S(2)}, u32[]{:S(2)}) async-start(s32[1,32,64]{2,0,1:T(1,128)} %reshape.1831), calls=%async_computation.13 | async-start | bytes 32768 | tf_op jit(solution)/shard_map/all_to_all | solution.py:95
  432.2 32.5 %collective-permute-start.1 = (f32[12,1024]{0,1:T(8,128)S(1)}, f32[12,1024]{0,1:T(8,128)S(1)}, u32[]{:S(2)}, u32[]{:S(2)}) collective-permute-start(f32[12,1024]{0,1:T(8,128)S(1)} %select_bitcast_fusion.4), channel_id=1, source_target_pairs={{480,0},{0,32},{32,64},{64,96},{96,128},{128,160},{160,192},{192,2... | collective-permute-start | bytes 147464 | tf_op jit(solution)/shard_map/ppermute | solution.py:12
  472.1 17.5 %all-to-all-start.12 = ((f32[32,1,768]{2,1,0:T(1,128)}), f32[32,1,768]{2,1,0:T(1,128)S(1)}, u32[]{:S(2)}, u32[]{:S(2)}) async-start(f32[32,1,768]{2,1,0:T(1,128)} %reshape.3410), calls=%async_computation.12 | async-start | bytes 196608 | tf_op jit(solution)/shard_map/all_to_all | solution.py:94
  489.5 12.4 %all-to-all-start.16 = ((s32[1,32,64]{2,0,1:T(1,128)}), s32[1,32,64]{2,0,1:T(1,128)S(1)}, u32[]{:S(2)}, u32[]{:S(2)}) async-start(s32[1,32,64]{2,0,1:T(1,128)} %reshape.1835), calls=%async_computation.16 | async-start | bytes 32768 | tf_op jit(solution)/shard_map/all_to_all | solution.py:95
  501.9 16.2 %all-to-all-start.14 = ((f32[32,1,768]{2,1,0:T(1,128)}), f32[32,1,768]{2,1,0:T(1,128)S(1)}, u32[]{:S(2)}, u32[]{:S(2)}) async-start(f32[32,1,768]{2,1,0:T(1,128)} %reshape.3412), calls=%async_computation.14 | async-start | bytes 196608 | tf_op jit(solution)/shard_map/all_to_all | solution.py:90
  529.9 12.3 %all-to-all-start.15 = ((f32[32,1,768]{2,1,0:T(1,128)}), f32[32,1,768]{2,1,0:T(1,128)S(1)}, u32[]{:S(2)}, u32[]{:S(2)}) async-start(f32[32,1,768]{2,1,0:T(1,128)} %reshape.3414), calls=%async_computation.15 | async-start | bytes 196608 | tf_op jit(solution)/shard_map/all_to_all | solution.py:94
  550.6 12.3 %all-to-all-start.17 = ((f32[32,1,768]{2,1,0:T(1,128)}), f32[32,1,768]{2,1,0:T(1,128)S(1)}, u32[]{:S(2)}, u32[]{:S(2)}) async-start(f32[32,1,768]{2,1,0:T(1,128)} %reshape.3416), calls=%async_computation.17 | async-start | bytes 196608 | tf_op jit(solution)/shard_map/all_to_all | solution.py:90
  562.9 21.4 %all-to-all-start.19 = ((s32[1,32,64]{2,0,1:T(1,128)}), s32[1,32,64]{2,0,1:T(1,128)S(1)}, u32[]{:S(2)}, u32[]{:S(2)}) async-start(s32[1,32,64]{2,0,1:T(1,128)} %reshape.1839), calls=%async_computation.19 | async-start | bytes 32768 | tf_op jit(solution)/shard_map/all_to_all | solution.py:95
  571.0 32.7 %collective-permute-start.2 = (f32[12,1024]{0,1:T(8,128)S(1)}, f32[12,1024]{0,1:T(8,128)S(1)}, u32[]{:S(2)}, u32[]{:S(2)}) collective-permute-start(f32[12,1024]{0,1:T(8,128)S(1)} %select_bitcast_fusion.2), channel_id=1, source_target_pairs={{480,0},{0,32},{32,64},{64,96},{96,128},{128,160},{160,192},{192,2... | collective-permute-start | bytes 147464 | tf_op jit(solution)/shard_map/ppermute | solution.py:12
  611.0 17.7 %all-to-all-start.18 = ((f32[32,1,768]{2,1,0:T(1,128)}), f32[32,1,768]{2,1,0:T(1,128)S(1)}, u32[]{:S(2)}, u32[]{:S(2)}) async-start(f32[32,1,768]{2,1,0:T(1,128)} %reshape.3418), calls=%async_computation.18 | async-start | bytes 196608 | tf_op jit(solution)/shard_map/all_to_all | solution.py:94
  628.7 12.2 %all-to-all-start.22 = ((s32[1,32,64]{2,0,1:T(1,128)}), s32[1,32,64]{2,0,1:T(1,128)S(1)}, u32[]{:S(2)}, u32[]{:S(2)}) async-start(s32[1,32,64]{2,0,1:T(1,128)} %reshape.1843), calls=%async_computation.22 | async-start | bytes 32768 | tf_op jit(solution)/shard_map/all_to_all | solution.py:95
  640.9 16.1 %all-to-all-start.20 = ((f32[32,1,768]{2,1,0:T(1,128)}), f32[32,1,768]{2,1,0:T(1,128)S(1)}, u32[]{:S(2)}, u32[]{:S(2)}) async-start(f32[32,1,768]{2,1,0:T(1,128)} %reshape.3420), calls=%async_computation.20 | async-start | bytes 196608 | tf_op jit(solution)/shard_map/all_to_all | solution.py:90
  668.8 12.3 %all-to-all-start.21 = ((f32[32,1,768]{2,1,0:T(1,128)}), f32[32,1,768]{2,1,0:T(1,128)S(1)}, u32[]{:S(2)}, u32[]{:S(2)}) async-start(f32[32,1,768]{2,1,0:T(1,128)} %reshape.3422), calls=%async_computation.21 | async-start | bytes 196608 | tf_op jit(solution)/shard_map/all_to_all | solution.py:94
  689.4 12.3 %all-to-all-start.23 = ((f32[32,1,768]{2,1,0:T(1,128)}), f32[32,1,768]{2,1,0:T(1,128)S(1)}, u32[]{:S(2)}, u32[]{:S(2)}) async-start(f32[32,1,768]{2,1,0:T(1,128)} %reshape.3424), calls=%async_computation.23 | async-start | bytes 196608 | tf_op jit(solution)/shard_map/all_to_all | solution.py:90
  706.1 33.6 %collective-permute-start.3 = (f32[12,1024]{0,1:T(8,128)S(1)}, f32[12,1024]{0,1:T(8,128)S(1)}, u32[]{:S(2)}, u32[]{:S(2)}) collective-permute-start(f32[12,1024]{0,1:T(8,128)S(1)} %select_bitcast_fusion), channel_id=1, source_target_pairs={{480,0},{0,32},{32,64},{64,96},{96,128},{128,160},{160,192},{192,2... | collective-permute-start | bytes 147464 | tf_op jit(solution)/shard_map/ppermute | solution.py:12
  (1 other events, 19.5 us)
where the time goes:
time: 755 us; the launch traced here: 741 us
  local copies, waits for them, and re-layouts  222 us (29%)
  waiting for transfers between devices  201 us (27%)
  starting transfers between devices  180 us (24%)
  other arithmetic  130 us (17%)
    gather x16, local copies, waits for them, and re-layouts, collect(): taken = jnp.take(values, source, axis=1)  112 us
    ppermute x4, waiting for transfers between devices, shifted(): return lax.ppermute(block, axis, route)  74.6 us
    another operation x16, other arithmetic  72.4 us
    all_to_all x8, waiting for transfers between devices, visit_whole(): return lax.all_to_all(moved, 'sky', split_axis=1, concat_axis=1, tiled=True)  64.4 us
    all_to_all x8, waiting for transfers between devices, body(): lax.all_to_all(sent, 'sky', split_axis=1, concat_axis=1, tiled=True)  61.8 us
    all_to_all x8, starting transfers between devices, body(): lax.all_to_all(sent, 'sky', split_axis=1, concat_axis=1, tiled=True)  50.6 us
    all_to_all x8, starting transfers between devices, visit_whole(): return lax.all_to_all(moved, 'sky', split_axis=1, concat_axis=1, tiled=True)  46.5 us
    ppermute x4, starting transfers between devices, shifted(): return lax.ppermute(block, axis, route)  45.5 us
  transfers between devices with their start and end apart: 28, of which 20 were waited for; matrix products, arithmetic and copies ran while one was open for 22% of the time, Pallas kernels for 0%

commit v1 on v0

v1 whole, which is shorter than its diff:
```python
import functools
import math

import jax
import jax.numpy as jnp
from jax import lax
from jax.experimental import pallas as pl
from jax.experimental.pallas import tpu as pltpu
from jax.sharding import PartitionSpec as P

RAYS = 1024
PATCHES = 256
HOPS = 4
TILES = 32
ROWS = 48
CHUNK = 256
GROUPS = RAYS // 128
VMEM = pl.BlockSpec(memory_space=pltpu.VMEM)
SMEM = pl.BlockSpec(memory_space=pltpu.SMEM)
PARAMS = pltpu.CompilerParams(vmem_limit_bytes=48 * 1024 * 1024)


def partner(axis, mask):
    shift = {"x": 3, "z": 1, "core": 0}[axis]
    return [(s, s ^ (mask << shift)) for s in range(TILES)]


def coefficients_kernel(defl_ref, shear_ref, out_ref):
    angle = lax.broadcasted_iota(jnp.int32, (8, PATCHES), 0)
    root = math.sqrt(0.5)
    cos_y, sin_y = jnp.zeros((8, PATCHES), jnp.float32), jnp.zeros((8, PATCHES), jnp.float32)
    for j, (c, s) in enumerate(
        [(1, 0), (root, root), (0, 1), (-root, root), (-1, 0), (-root, -root), (0, -1), (root, -root)]
    ):
        cos_y = jnp.where(angle == j, c, cos_y)
        sin_y = jnp.where(angle == j, s, sin_y)
    for plane in range(2):
        for k in range(5):
            source, first = (defl_ref, k * 32) if k < 2 else (shear_ref, (k - 2) * 32)
            cells = source[0, plane, first : first + 32, :].astype(jnp.float32) * (1.0 / 32.0)
            r0, r1, r2, r3 = [cells[i * 8 : i * 8 + 8] for i in range(4)]
            for a, part in enumerate((r0 + r1 + r2 + r3, r0 - r2, r1 - r3)):
                row = plane * ROWS + k * 9 + a * 3
                out_ref[row : row + 1, :] = jnp.sum(part, axis=0, keepdims=True)
                out_ref[row + 1 : row + 2, :] = jnp.sum(part * cos_y, axis=0, keepdims=True)
                out_ref[row + 2 : row + 3, :] = jnp.sum(part * sin_y, axis=0, keepdims=True)
        out_ref[plane * ROWS + 45 : plane * ROWS + 48, :] = jnp.zeros((3, PATCHES), jnp.float32)


def coefficients(deflection, shear):
    return pl.pallas_call(
        coefficients_kernel,
        out_shape=jax.ShapeDtypeStruct((2 * ROWS, PATCHES), jnp.float32),
        in_specs=[VMEM] * 2,
        out_specs=VMEM,
        name="coefficients",
    )(deflection, shear)


def find_rows(hop, table_ref, rel_ref, patch_ref, out_ref):
    for plane in range(2):
        for chunk in range(RAYS // CHUNK):
            lanes = slice(chunk * CHUNK, (chunk + 1) * CHUNK)
            row = hop * 2 + plane
            patch = patch_ref[row : row + 1, lanes]
            rel = rel_ref[row : row + 1, lanes]
            onehot = lax.broadcasted_iota(jnp.int32, (PATCHES, CHUNK), 0) == patch
            onehot = jnp.where(onehot, 1.0, 0.0).astype(jnp.bfloat16)
            onehot = jnp.concatenate([onehot, onehot], axis=0)
            found = jnp.dot(table_ref[plane], onehot, preferred_element_type=jnp.float32)
            total = [jnp.zeros((8, CHUNK), jnp.float32) for _ in range(ROWS // 8)]
            wide = jnp.broadcast_to(rel, (8, CHUNK))
            for tile in range(TILES):
                here = wide == tile
                for part in range(ROWS // 8):
                    first = tile * ROWS + part * 8
                    total[part] = total[part] + jnp.where(here, found[first : first + 8], 0.0)
            for part in range(ROWS // 8):
                for half in range(CHUNK // 128):
                    group = chunk * (CHUNK // 128) + half
                    first = (plane * ROWS + part * 8) * GROUPS + group
                    out_ref[pl.ds(first, 8, stride=GROUPS), :] = total[part][:, half * 128 : half * 128 + 128]


def first_lookup_kernel(own_ref, other_ref, rel_ref, patch_ref, out_ref, table_ref):
    for core, ref in enumerate((own_ref, other_ref)):
        for block in range(TILES // 2):
            tile = block * 2 + core
            for plane in range(2):
                values = ref[block, plane * ROWS : (plane + 1) * ROWS, :]
                high = values.astype(jnp.bfloat16)
                low = (values - high.astype(jnp.float32)).astype(jnp.bfloat16)
                table_ref[plane, tile * ROWS : (tile + 1) * ROWS, :PATCHES] = high
                table_ref[plane, tile * ROWS : (tile + 1) * ROWS, PATCHES:] = low
    find_rows(0, table_ref, rel_ref, patch_ref, out_ref)


COST = pl.CostEstimate(flops=2 * 2 * TILES * ROWS * 512 * RAYS, bytes_accessed=4 * 1024 * 1024, transcendentals=0)
FOUND = jax.ShapeDtypeStruct((2 * ROWS * GROUPS, 128), jnp.float32)


def first_lookup(own, other, rel, patch):
    return pl.pallas_call(
        first_lookup_kernel,
        out_shape=(FOUND, jax.ShapeDtypeStruct((2, TILES * ROWS, 2 * PATCHES), jnp.bfloat16)),
        in_specs=[VMEM] * 4,
        out_specs=(VMEM, VMEM),
        compiler_params=PARAMS,
        cost_estimate=COST,
        name="first_lookup",
    )(own, other, rel, patch)


def lookup(hop, table, rel, patch):
    return pl.pallas_call(
        functools.partial(find_rows, hop),
        out_shape=FOUND,
        in_specs=[VMEM] * 3,
        out_specs=VMEM,
        compiler_params=PARAMS,
        cost_estimate=COST,
        name="lookup",
    )(table, rel, patch)


def sine(turn):
    v = turn * (2.0 * math.pi)
    v2 = v * v
    poly = 1.0 / 6227020800.0
    for c in (-1.0 / 39916800.0, 1.0 / 362880.0, -1.0 / 5040.0, 1.0 / 120.0, -1.0 / 6.0):
        poly = poly * v2 + c
    return v + v * v2 * poly


def wave(turns):
    t = turns - jnp.floor(turns + 0.5)
    size = jnp.abs(t)
    fold = jnp.where(t >= 0, 0.5 - t, -0.5 - t)
    return sine(0.25 - size), sine(jnp.where(size > 0.25, fold, t))


def advance(state, read):
    pos_x, pos_y, ang_x, ang_y, a11, a12, a21, a22, b11, b12, b21, b22 = state
    cos_x, sin_x = wave(pos_x * 0.25)
    cos_y, sin_y = wave(pos_y * 0.125)
    values = []
    for k in range(5):
        parts = []
        for a in range(3):
            m = [read(k * 9 + a * 3 + b) for b in range(3)]
            parts.append(m[0] + m[1] * cos_y + m[2] * sin_y)
        values.append(parts[0] + parts[1] * cos_x + parts[2] * sin_x)
    alpha_x, alpha_y, psi11, psi12, psi22 = values
    ang_x = ang_x - alpha_x
    ang_y = ang_y - alpha_y
    b11 = b11 - (psi11 * a11 + psi12 * a21)
    b12 = b12 - (psi11 * a12 + psi12 * a22)
    b21 = b21 - (psi12 * a11 + psi22 * a21)
    b22 = b22 - (psi12 * a12 + psi22 * a22)
    pos_x = pos_x + 0.5 * ang_x
    pos_y = pos_y + 0.5 * ang_y
    a11 = a11 + 0.5 * b11
    a12 = a12 + 0.5 * b12
    a21 = a21 + 0.5 * b21
    a22 = a22 + 0.5 * b22
    return [pos_x, pos_y, ang_x, ang_y, a11, a12, a21, a22, b11, b12, b21, b22]


def step_kernel(step, q_ref, *refs):
    *refs, out_ref = refs
    q = q_ref[0]
    refs = list(refs)
    main_ref = refs.pop(0)
    wrap_ref = refs.pop(0) if step >= 2 else None
    early_ref = refs.pop(0) if step < HOPS else None
    late_ref = refs.pop(0) if step >= 2 else None
    shape = (GROUPS, 128)
    late = jnp.full(shape, q, jnp.int32) < step
    crossed = jnp.full(shape, q, jnp.int32) == 0

    def rows(ref, k):
        return ref[k * GROUPS : (k + 1) * GROUPS, :]

    state = [rows(main_ref, k) for k in range(12)]
    if wrap_ref is not None:
        state = [jnp.where(crossed, rows(wrap_ref, k), state[k]) for k in range(12)]
    for plane in range(2):

        def read(k, plane=plane):
            k = plane * ROWS + k
            if early_ref is None:
                return rows(late_ref, k)
            if late_ref is None:
                return rows(early_ref, k)
            return jnp.where(late, rows(late_ref, k), rows(early_ref, k))

        state = advance(state, read)
    for k in range(12):
        out_ref[k * GROUPS : (k + 1) * GROUPS, :] = state[k]


def run_step(step, q, main, wrap, found):
    args = [main]
    if step >= 2:
        args.append(wrap)
    if step < HOPS:
        args.append(found[step])
    if step >= 2:
        args.append(found[step - 1])
    return pl.pallas_call(
        functools.partial(step_kernel, step),
        out_shape=jax.ShapeDtypeStruct((12 * GROUPS, 128), jnp.float32),
        in_specs=[SMEM] + [VMEM] * len(args),
        out_specs=VMEM,
        cost_estimate=pl.CostEstimate(flops=400 * RAYS, bytes_accessed=500 * 1024, transcendentals=0),
        name="step",
    )(q, *args)


def gather_tables(own):
    column = jnp.stack([own] + [lax.ppermute(own, "sky", partner("z", m)) for m in (1, 2, 3)])
    whole = jnp.concatenate([column] + [lax.ppermute(column, "sky", partner("x", m)) for m in (1, 2, 3)])
    return whole, lax.ppermute(whole, "sky", partner("core", 1))


def body(state, deflection, shear, routes, patches):
    slabs = lax.axis_size("los")
    run = slabs // 2
    slab = lax.axis_index("los")
    q = (slab % run).astype(jnp.int32).reshape(1)
    onward = [(i, i + 1) for i in range(slabs - 1) if i % run != run - 1]
    across = [(i, (i + 1) % slabs) for i in range(slabs) if i % run == run - 1]

    own = coefficients(deflection, shear)
    whole, other = gather_tables(own)
    rel = jnp.bitwise_xor(routes.reshape(2 * HOPS, RAYS), lax.axis_index("sky").astype(jnp.int32))
    patch = patches.reshape(2 * HOPS, RAYS)
    found = [None] * HOPS
    found[0], table = first_lookup(whole, other, rel, patch)
    main, wraps = state.reshape(12 * GROUPS, 128), []
    for step in range(HOPS + 1):
        if 0 < step < HOPS:
            found[step] = lookup(step, table, rel, patch)
        moved = run_step(step, q, main, wraps[step - 2] if step >= 2 else None, found)
        arrived = lax.ppermute(moved, "los", onward)
        if step < HOPS:
            wraps.append(lax.ppermute(moved, "los", across))
        before, main = main, arrived
    out = jnp.where(q[0] == 0, wraps[HOPS - 1], jnp.where(q[0] < HOPS, main, before))
    return out.reshape(12, RAYS)


def solution(mesh):
    placed = (
        P(None, ("los", "sky")),
        P("los", None, None, "sky"),
        P("los", None, None, "sky"),
        P(None, None, ("los", "sky"), None),
        P(None, None, ("los", "sky")),
    )
    return jax.shard_map(
        body, mesh=mesh, in_specs=placed, out_specs=P(None, ("los", "sky")), check_vma=False
    )
```

time: 755 us -> 122 us (0.16); the launches traced: 741 us -> 121 us
  local copies, waits for them, and re-layouts: 222 us -> 10.9 us
  waiting for transfers between devices: 201 us -> 31.1 us
  starting transfers between devices: 180 us -> 51 us
  other arithmetic: 130 us -> 1.83 us
  Pallas kernels: 0 us -> 25.6 us
    gather x24 -> x0, local copies, waits for them, and re-layouts: 135 us -> none  [the longest x16 112 us: collect(): taken = jnp.take(values, source, axis=1)]
    all_to_all x24 -> x0, starting transfers between devices: 134 us -> none  [the longest x8 50.6 us: body(): lax.all_to_all(sent, 'sky', split_axis=1, concat_axis=1, tiled=True)]
    all_to_all x24 -> x0, waiting for transfers between devices: 126 us -> none  [the longest x8 64.4 us: visit_whole(): return lax.all_to_all(moved, 'sky', split_axis=1, concat_axis=1, tiled=True)]
    another operation x16 -> x1, other arithmetic: 72.4 us -> 0.92 us  [gather_tables(): jnp.stack([own] + [lax.ppermute(own, 'sky', partner('z', m)) for m in (1,...]
    ppermute x4 -> x16, waiting for transfers between devices: 74.6 us -> 31.1 us  [the longest x3 17.1 us: gather_tables(): lax.ppermute(column, 'sky', partner('x', m))]
    scatter x8 -> x0, local copies, waits for them, and re-layouts: 34.7 us -> none  [arrange(): source = source.at[slot].set(jnp.arange(ray_count, dtype=jnp.int32))]
    pallas_call x0 -> x10, Pallas kernels: none -> 25.6 us  [the longest x3 10.5 us: lookup(): pl.pallas_call(functools.partial(find_rows, hop), out_shape=FOUND, in_spe...]
    sub x46 -> x0, other arithmetic: 23.7 us -> none  [the longest x8 5.83 us: advance(): b21 = b21 - (psi12 * a11 + psi22 * a21)]
  transfers between devices with their start and end apart: 28 -> 16, of which waited for: 20 -> 8; matrix products, arithmetic and copies ran while one was open for 22% -> 1% of each run, Pallas kernels for 0% -> 15%
where the time goes in v1:
time: 122 us; the launch traced here: 121 us
  starting transfers between devices  51 us (42%)
  waiting for transfers between devices  31.1 us (25%)
  Pallas kernels  25.6 us (21%)
  local copies, waits for them, and re-layouts  10.9 us (9%)
  other arithmetic  1.83 us (2%)
    ppermute x4, starting transfers between devices, body(): wraps.append(lax.ppermute(moved, 'los', across))  19.4 us
    ppermute x3, waiting for transfers between devices, gather_tables(): lax.ppermute(column, 'sky', partner('x', m))  17.1 us
    ppermute x3, starting transfers between devices, gather_tables(): lax.ppermute(own, 'sky', partner('z', m))  12.3 us
    ppermute x3, starting transfers between devices, gather_tables(): lax.ppermute(column, 'sky', partner('x', m))  10.6 us
    pallas_call x3, Pallas kernels, lookup(): pl.pallas_call(functools.partial(find_rows, hop), out_shape=FOUND, in_spe...  10.5 us
    unnamed x42, local copies, waits for them, and re-layouts  9.56 us
    pallas_call x5, Pallas kernels, run_step(): pl.pallas_call(functools.partial(step_kernel, step), out_shape=jax.ShapeD...  8.91 us
    ppermute x5, starting transfers between devices, body(): arrived = lax.ppermute(moved, 'los', onward)  6.84 us
  transfers between devices with their start and end apart: 16, of which 8 were waited for; matrix products, arithmetic and copies ran while one was open for 1% of the time, Pallas kernels for 15%

profile of v1, /device:TPU:56, one launch (start us, length us, event | category | flops | bytes accessed | tf_op | source)
XLA Modules:
  0.0 120.8 jit_solution(952466021787681448)
XLA Ops:
  0.0 1.8 %coefficients.1 = f32[96,256]{1,0:T(8,128)} custom-call(bf16[1,2,64,256]{3,2,1,0:T(8,128)(2,1)} %defl_ref.1, bf16[1,2,96,256]{3,2,1,0:T(8,128)(2,1)} %shear_ref.1), custom_call_target="tpu_custom_call" | custom-call | tf_op jit(solution)/shard_map/coefficients/pallas_call | solution.py:51
  1.8 4.3 %collective-permute-start = (f32[96,256]{1,0:T(8,128)}, f32[96,256]{1,0:T(8,128)S(1)}, u32[]{:S(2)}, u32[]{:S(2)}) collective-permute-start(f32[96,256]{1,0:T(8,128)} %coefficients.1), channel_id=1, source_target_pairs={{0,2},{1,3},{2,0},{3,1},{4,6},{5,7},{6,4},{7,5},{8,10},{9,11},{10,... | collective-permute-start | bytes 294920 | tf_op jit(solution)/shard_map/ppermute | solution.py:221
  6.1 6.1 %collective-permute-start.1 = (f32[96,256]{1,0:T(8,128)}, f32[96,256]{1,0:T(8,128)S(1)}, u32[]{:S(2)}, u32[]{:S(2)}) collective-permute-start(f32[96,256]{1,0:T(8,128)} %coefficients.1), channel_id=1, source_target_pairs={{0,4},{1,5},{2,6},{3,7},{4,0},{5,1},{6,2},{7,3},{8,12},{9,13},{10,... | collective-permute-start | bytes 294920 | tf_op jit(solution)/shard_map/ppermute | solution.py:221
  12.2 1.9 %collective-permute-start.2 = (f32[96,256]{1,0:T(8,128)}, f32[96,256]{1,0:T(8,128)S(1)}, u32[]{:S(2)}, u32[]{:S(2)}) collective-permute-start(f32[96,256]{1,0:T(8,128)} %coefficients.1), channel_id=1, source_target_pairs={{0,6},{1,7},{2,4},{3,5},{4,2},{5,3},{6,0},{7,1},{8,14},{9,15},{10,... | collective-permute-start | bytes 294920 | tf_op jit(solution)/shard_map/ppermute | solution.py:221
  15.0 2.0 %collective-permute-done.1 = f32[96,256]{1,0:T(8,128)S(1)} collective-permute-done((f32[96,256]{1,0:T(8,128)}, f32[96,256]{1,0:T(8,128)S(1)}, u32[]{:S(2)}, u32[]{:S(2)}) %collective-permute-start.1) | collective-permute-done | bytes 98336 | tf_op jit(solution)/shard_map/ppermute | solution.py:221
  17.0 3.8 %collective-permute-done.2 = f32[96,256]{1,0:T(8,128)S(1)} collective-permute-done((f32[96,256]{1,0:T(8,128)}, f32[96,256]{1,0:T(8,128)S(1)}, u32[]{:S(2)}, u32[]{:S(2)}) %collective-permute-start.2) | collective-permute-done | bytes 98336 | tf_op jit(solution)/shard_map/ppermute | solution.py:221
  21.8 3.5 %collective-permute-start.3 = (f32[4,96,256]{2,1,0:T(8,128)S(1)}, f32[4,96,256]{2,1,0:T(8,128)S(1)}, u32[]{:S(2)}, u32[]{:S(2)}) collective-permute-start(f32[4,96,256]{2,1,0:T(8,128)S(1)} %pad_maximum_fusion), channel_id=1, source_target_pairs={{0,8},{1,9},{2,10},{3,11},{4,12},{5,13},{6,14},{7,15},{8,0},{9,1},... | collective-permute-start | bytes 1179656 | tf_op jit(solution)/shard_map/ppermute | solution.py:222
  25.3 4.6 %collective-permute-start.4 = (f32[4,96,256]{2,1,0:T(8,128)S(1)}, f32[4,96,256]{2,1,0:T(8,128)S(1)}, u32[]{:S(2)}, u32[]{:S(2)}) collective-permute-start(f32[4,96,256]{2,1,0:T(8,128)S(1)} %pad_maximum_fusion), channel_id=1, source_target_pairs={{0,16},{1,17},{2,18},{3,19},{4,20},{5,21},{6,22},{7,23},{8,24},{9,... | collective-permute-start | bytes 1179656 | tf_op jit(solution)/shard_map/ppermute | solution.py:222
  29.9 2.4 %collective-permute-start.5 = (f32[4,96,256]{2,1,0:T(8,128)S(1)}, f32[4,96,256]{2,1,0:T(8,128)S(1)}, u32[]{:S(2)}, u32[]{:S(2)}) collective-permute-start(f32[4,96,256]{2,1,0:T(8,128)S(1)} %pad_maximum_fusion), channel_id=1, source_target_pairs={{0,24},{1,25},{2,26},{3,27},{4,28},{5,29},{6,30},{7,31},{8,16},{9,... | collective-permute-start | bytes 1179656 | tf_op jit(solution)/shard_map/ppermute | solution.py:222
  32.4 3.4 %collective-permute-done.3 = f32[4,96,256]{2,1,0:T(8,128)S(1)} collective-permute-done((f32[4,96,256]{2,1,0:T(8,128)S(1)}, f32[4,96,256]{2,1,0:T(8,128)S(1)}, u32[]{:S(2)}, u32[]{:S(2)}) %collective-permute-start.3) | collective-permute-done | bytes 393248 | tf_op jit(solution)/shard_map/ppermute | solution.py:222
  35.9 7.8 %collective-permute-done.4 = f32[4,96,256]{2,1,0:T(8,128)S(1)} collective-permute-done((f32[4,96,256]{2,1,0:T(8,128)S(1)}, f32[4,96,256]{2,1,0:T(8,128)S(1)}, u32[]{:S(2)}, u32[]{:S(2)}) %collective-permute-start.4) | collective-permute-done | bytes 393248 | tf_op jit(solution)/shard_map/ppermute | solution.py:222
  43.7 5.9 %collective-permute-done.5 = f32[4,96,256]{2,1,0:T(8,128)S(1)} collective-permute-done((f32[4,96,256]{2,1,0:T(8,128)S(1)}, f32[4,96,256]{2,1,0:T(8,128)S(1)}, u32[]{:S(2)}, u32[]{:S(2)}) %collective-permute-start.5) | collective-permute-done | bytes 393248 | tf_op jit(solution)/shard_map/ppermute | solution.py:222
  49.6 1.9 %collective-permute-start.6 = (f32[16,96,256]{2,1,0:T(8,128)S(1)}, f32[16,96,256]{2,1,0:T(8,128)S(1)}, u32[]{:S(2)}, u32[]{:S(2)}) collective-permute-start(f32[16,96,256]{2,1,0:T(8,128)S(1)} %constant_dynamic-update-slice_fusion.own_ref), channel_id=1, source_target_pairs={{0,1},{1,0},{2,3},{3,2},{4,5},{5,4},{6,7},{7,6},{8,9},{9,8},{10,11... | collective-permute-start | bytes 4718600 | tf_op jit(solution)/shard_map/ppermute | solution.py:223
  52.4 2.5 %collective-permute-done.6.other_ref = f32[16,96,256]{2,1,0:T(8,128)S(1)} collective-permute-done((f32[16,96,256]{2,1,0:T(8,128)S(1)}, f32[16,96,256]{2,1,0:T(8,128)S(1)}, u32[]{:S(2)}, u32[]{:S(2)}) %collective-permute-start.6) | collective-permute-done | bytes 1572896 | tf_op jit(solution)/shard_map/ppermute | solution.py:223
  54.9 4.4 %first_lookup.1 = (f32[768,128]{1,0:T(8,128)S(1)}, bf16[2,1536,512]{2,1,0:T(8,128)(2,1)}) custom-call(f32[16,96,256]{2,1,0:T(8,128)S(1)} %constant_dynamic-update-slice_fusion.own_ref, f32[16,96,256]{2,1,0:T(8,128)S(1)} %collective-permute-done.6.other_ref, s32[8,1024]{1,0:T(8,128)S(1)} %xor.10.rel_ref, s32[8,1024]{1,0:T(8,128)S(1)} %reshape.17.patch_ref), custom_call_target="tpu_custom_call" | custom-call | flops 3221225472 | bytes 4194304 | tf_op jit(solution)/shard_map/first_lookup/pallas_call | solution.py:103
  60.0 1.7 %step.5 = f32[96,128]{1,0:T(8,128)} custom-call(s32[1]{0:T(128)} %bitcast.q_ref, f32[96,128]{1,0:T(8,128)} %reshape.16.refs_0_, f32[768,128]{1,0:T(8,128)} %copy-done.3), custom_call_target="tpu_custom_call" | custom-call | flops 409600 | bytes 512000 | tf_op jit(solution)/shard_map/step/pallas_call | solution.py:210
  61.7 1.3 %collective-permute-start.7 = (f32[96,128]{1,0:T(8,128)}, f32[96,128]{1,0:T(8,128)S(1)}, u32[]{:S(2)}, u32[]{:S(2)}) collective-permute-start(f32[96,128]{1,0:T(8,128)} %step.5), channel_id=1, source_target_pairs={{0,32},{32,64},{64,96},{96,128},{128,160},{160,192},{192,224},{256... | collective-permute-start | bytes 147464 | tf_op jit(solution)/shard_map/ppermute | solution.py:245
  63.0 9.6 %collective-permute-start.9 = (f32[96,128]{1,0:T(8,128)}, f32[96,128]{1,0:T(8,128)S(1)}, u32[]{:S(2)}, u32[]{:S(2)}) collective-permute-start(f32[96,128]{1,0:T(8,128)} %step.5), channel_id=1, source_target_pairs={{224,256},{480,0},{225,257},{481,1},{226,258},{482,2},{227,259},{4... | collective-permute-start | bytes 147464 | tf_op jit(solution)/shard_map/ppermute | solution.py:247
  72.7 1.9 %copy-done.4 = bf16[2,1536,512]{2,1,0:T(8,128)(2,1)S(1)} copy-done((bf16[2,1536,512]{2,1,0:T(8,128)(2,1)S(1)}, bf16[2,1536,512]{2,1,0:T(8,128)(2,1)}, u32[]{:S(2)}) %copy-start.4) | copy-done | bytes 3145752
  74.5 3.5 %lookup.3.refs_1_.refs_3_ = f32[768,128]{1,0:T(8,128)S(1)} custom-call(bf16[2,1536,512]{2,1,0:T(8,128)(2,1)S(1)} %copy-done.4, s32[8,1024]{1,0:T(8,128)S(1)} %xor.10.rel_ref, s32[8,1024]{1,0:T(8,128)S(1)} %reshape.17.patch_ref), custom_call_target="tpu_custom_call" | custom-call | flops 3221225472 | bytes 4194304 | tf_op jit(solution)/shard_map/lookup/pallas_call | solution.py:115
  79.4 1.7 %step.6 = f32[96,128]{1,0:T(8,128)} custom-call(s32[1]{0:T(128)} %bitcast.q_ref, f32[96,128]{1,0:T(8,128)} %copy-done.15, f32[768,128]{1,0:T(8,128)} %copy-done.2), custom_call_target="tpu_custom_call" | custom-call | flops 409600 | bytes 512000 | tf_op jit(solution)/shard_map/step/pallas_call | solution.py:210
  81.1 1.4 %collective-permute-start.8 = (f32[96,128]{1,0:T(8,128)}, f32[96,128]{1,0:T(8,128)S(1)}, u32[]{:S(2)}, u32[]{:S(2)}) collective-permute-start(f32[96,128]{1,0:T(8,128)} %step.6), channel_id=1, source_target_pairs={{0,32},{32,64},{64,96},{96,128},{128,160},{160,192},{192,224},{256... | collective-permute-start | bytes 147464 | tf_op jit(solution)/shard_map/ppermute | solution.py:245
  82.5 3.5 %lookup.4.refs_2_.refs_3_ = f32[768,128]{1,0:T(8,128)S(1)} custom-call(bf16[2,1536,512]{2,1,0:T(8,128)(2,1)S(1)} %copy-done.5, s32[8,1024]{1,0:T(8,128)S(1)} %xor.10.rel_ref, s32[8,1024]{1,0:T(8,128)S(1)} %reshape.17.patch_ref), custom_call_target="tpu_custom_call" | custom-call | flops 3221225472 | bytes 4194304 | tf_op jit(solution)/shard_map/lookup/pallas_call | solution.py:115
  86.8 2.8 %collective-permute-start.11 = (f32[96,128]{1,0:T(8,128)S(1)}, f32[96,128]{1,0:T(8,128)S(1)}, u32[]{:S(2)}, u32[]{:S(2)}) collective-permute-start(f32[96,128]{1,0:T(8,128)S(1)} %copy-done.13), channel_id=1, source_target_pairs={{224,256},{480,0},{225,257},{481,1},{226,258},{482,2},{227,259},{4... | collective-permute-start | bytes 147464 | tf_op jit(solution)/shard_map/ppermute | solution.py:247
  90.9 1.9 %step.7 = f32[96,128]{1,0:T(8,128)} custom-call(s32[1]{0:T(128)} %bitcast.q_ref, f32[96,128]{1,0:T(8,128)} %copy-done.12, f32[96,128]{1,0:T(8,128)} %copy-done.10, f32[768,128]{1,0:T(8,128)} %copy-done, f32[768,128]{1,0:T(8,128)} %copy-done.2), custom_call_target="tpu_custom_call" | custom-call | flops 409600 | bytes 512000 | tf_op jit(solution)/shard_map/step/pallas_call | solution.py:210
  92.8 1.6 %collective-permute-start.10 = (f32[96,128]{1,0:T(8,128)}, f32[96,128]{1,0:T(8,128)S(1)}, u32[]{:S(2)}, u32[]{:S(2)}) collective-permute-start(f32[96,128]{1,0:T(8,128)} %step.7), channel_id=1, source_target_pairs={{0,32},{32,64},{64,96},{96,128},{128,160},{160,192},{192,224},{256... | collective-permute-start | bytes 147464 | tf_op jit(solution)/shard_map/ppermute | solution.py:245
  94.4 3.5 %lookup.5.refs_2_ = f32[768,128]{1,0:T(8,128)S(1)} custom-call(bf16[2,1536,512]{2,1,0:T(8,128)(2,1)S(1)} %copy-done.5, s32[8,1024]{1,0:T(8,128)S(1)} %xor.10.rel_ref, s32[8,1024]{1,0:T(8,128)S(1)} %reshape.17.patch_ref), custom_call_target="tpu_custom_call" | custom-call | flops 3221225472 | bytes 4194304 | tf_op jit(solution)/shard_map/lookup/pallas_call | solution.py:115
  98.6 2.8 %collective-permute-start.14 = (f32[96,128]{1,0:T(8,128)S(1)}, f32[96,128]{1,0:T(8,128)S(1)}, u32[]{:S(2)}, u32[]{:S(2)}) collective-permute-start(f32[96,128]{1,0:T(8,128)S(1)} %copy-done.8), channel_id=1, source_target_pairs={{224,256},{480,0},{225,257},{481,1},{226,258},{482,2},{227,259},{4... | collective-permute-start | bytes 147464 | tf_op jit(solution)/shard_map/ppermute | solution.py:247
  102.7 1.9 %step.8 = f32[96,128]{1,0:T(8,128)} custom-call(s32[1]{0:T(128)} %bitcast.q_ref, f32[96,128]{1,0:T(8,128)} %copy-done.11, f32[96,128]{1,0:T(8,128)} %copy-done.9, f32[768,128]{1,0:T(8,128)} %copy-done.1, f32[768,128]{1,0:T(8,128)} %copy-done), custom_call_target="tpu_custom_call" | custom-call | flops 409600 | bytes 512000 | tf_op jit(solution)/shard_map/step/pallas_call | solution.py:210
  105.9 4.1 %collective-permute-start.12 = (f32[96,128]{1,0:T(8,128)}, f32[96,128]{1,0:T(8,128)S(1)}, u32[]{:S(2)}, u32[]{:S(2)}) collective-permute-start(f32[96,128]{1,0:T(8,128)} %step.8), channel_id=1, source_target_pairs={{224,256},{480,0},{225,257},{481,1},{226,258},{482,2},{227,259},{4... | collective-permute-start | bytes 147464 | tf_op jit(solution)/shard_map/ppermute | solution.py:247
  111.4 1.7 %step.9 = f32[96,128]{1,0:T(8,128)} custom-call(s32[1]{0:T(128)} %bitcast.q_ref, f32[96,128]{1,0:T(8,128)} %copy-done.6, f32[96,128]{1,0:T(8,128)} %copy-done.14, f32[768,128]{1,0:T(8,128)} %copy-done.1), custom_call_target="tpu_custom_call" | custom-call | flops 409600 | bytes 512000 | tf_op jit(solution)/shard_map/step/pallas_call | solution.py:210
  114.5 4.9 %collective-permute-done.15 = f32[96,128]{1,0:T(8,128)S(1)} collective-permute-done((f32[96,128]{1,0:T(8,128)}, f32[96,128]{1,0:T(8,128)S(1)}, u32[]{:S(2)}, u32[]{:S(2)}) %collective-permute-start.15) | collective-permute-done | bytes 49184 | tf_op jit(solution)/shard_map/ppermute | solution.py:245
  (60 shorter events, 14.2 us)
Async XLA Ops:
  1.8 13.2 %collective-permute-start = (f32[96,256]{1,0:T(8,128)}, f32[96,256]{1,0:T(8,128)S(1)}, u32[]{:S(2)}, u32[]{:S(2)}) collective-permute-start(f32[96,256]{1,0:T(8,128)} %coefficients.1), channel_id=1, source_target_pairs={{0,2},{1,3},{2,0},{3,1},{4,6},{5,7},{6,4},{7,5},{8,10},{9,11},{10,... | collective-permute-start | bytes 294920 | tf_op jit(solution)/shard_map/ppermute | solution.py:221
  6.1 10.9 %collective-permute-start.1 = (f32[96,256]{1,0:T(8,128)}, f32[96,256]{1,0:T(8,128)S(1)}, u32[]{:S(2)}, u32[]{:S(2)}) collective-permute-start(f32[96,256]{1,0:T(8,128)} %coefficients.1), channel_id=1, source_target_pairs={{0,4},{1,5},{2,6},{3,7},{4,0},{5,1},{6,2},{7,3},{8,12},{9,13},{10,... | collective-permute-start | bytes 294920 | tf_op jit(solution)/shard_map/ppermute | solution.py:221
  12.2 8.6 %collective-permute-start.2 = (f32[96,256]{1,0:T(8,128)}, f32[96,256]{1,0:T(8,128)S(1)}, u32[]{:S(2)}, u32[]{:S(2)}) collective-permute-start(f32[96,256]{1,0:T(8,128)} %coefficients.1), channel_id=1, source_target_pairs={{0,6},{1,7},{2,4},{3,5},{4,2},{5,3},{6,0},{7,1},{8,14},{9,15},{10,... | collective-permute-start | bytes 294920 | tf_op jit(solution)/shard_map/ppermute | solution.py:221
  21.7 29.8 %copy-start.16 = (s32[4,2,1024,1]{2,3,1,0:T(1,128)S(1)}, s32[4,2,1024,1]{2,3,1,0:T(1,128)}, u32[]{:S(2)}) copy-start(s32[4,2,1024,1]{2,3,1,0:T(1,128)} %param.8) | copy-start | bytes 98308
  21.7 29.9 %copy-start.17 = (s32[4,2,1024]{2,1,0:T(2,128)S(1)}, s32[4,2,1024]{2,1,0:T(2,128)}, u32[]{:S(2)}) copy-start(s32[4,2,1024]{2,1,0:T(2,128)} %param.9) | copy-start | bytes 98308
  21.7 30.0 %copy-start.7 = (f32[12,1024]{1,0:T(8,128)S(1)}, f32[12,1024]{1,0:T(8,128)}, u32[]{:S(2)}) copy-start(f32[12,1024]{1,0:T(8,128)} %param.5) | copy-start | bytes 147460
  21.8 14.1 %collective-permute-start.3 = (f32[4,96,256]{2,1,0:T(8,128)S(1)}, f32[4,96,256]{2,1,0:T(8,128)S(1)}, u32[]{:S(2)}, u32[]{:S(2)}) collective-permute-start(f32[4,96,256]{2,1,0:T(8,128)S(1)} %pad_maximum_fusion), channel_id=1, source_target_pairs={{0,8},{1,9},{2,10},{3,11},{4,12},{5,13},{6,14},{7,15},{8,0},{9,1},... | collective-permute-start | bytes 1179656 | tf_op jit(solution)/shard_map/ppermute | solution.py:222
  25.3 18.4 %collective-permute-start.4 = (f32[4,96,256]{2,1,0:T(8,128)S(1)}, f32[4,96,256]{2,1,0:T(8,128)S(1)}, u32[]{:S(2)}, u32[]{:S(2)}) collective-permute-start(f32[4,96,256]{2,1,0:T(8,128)S(1)} %pad_maximum_fusion), channel_id=1, source_target_pairs={{0,16},{1,17},{2,18},{3,19},{4,20},{5,21},{6,22},{7,23},{8,24},{9,... | collective-permute-start | bytes 1179656 | tf_op jit(solution)/shard_map/ppermute | solution.py:222
  29.9 19.6 %collective-permute-start.5 = (f32[4,96,256]{2,1,0:T(8,128)S(1)}, f32[4,96,256]{2,1,0:T(8,128)S(1)}, u32[]{:S(2)}, u32[]{:S(2)}) collective-permute-start(f32[4,96,256]{2,1,0:T(8,128)S(1)} %pad_maximum_fusion), channel_id=1, source_target_pairs={{0,24},{1,25},{2,26},{3,27},{4,28},{5,29},{6,30},{7,31},{8,16},{9,... | collective-permute-start | bytes 1179656 | tf_op jit(solution)/shard_map/ppermute | solution.py:222
  49.6 5.3 %collective-permute-start.6 = (f32[16,96,256]{2,1,0:T(8,128)S(1)}, f32[16,96,256]{2,1,0:T(8,128)S(1)}, u32[]{:S(2)}, u32[]{:S(2)}) collective-permute-start(f32[16,96,256]{2,1,0:T(8,128)S(1)} %constant_dynamic-update-slice_fusion.own_ref), channel_id=1, source_target_pairs={{0,1},{1,0},{2,3},{3,2},{4,5},{5,4},{6,7},{7,6},{8,9},{9,8},{10,11... | collective-permute-start | bytes 4718600 | tf_op jit(solution)/shard_map/ppermute | solution.py:223
  59.3 0.7 copy-start.3
  61.7 17.0 %collective-permute-start.7 = (f32[96,128]{1,0:T(8,128)}, f32[96,128]{1,0:T(8,128)S(1)}, u32[]{:S(2)}, u32[]{:S(2)}) collective-permute-start(f32[96,128]{1,0:T(8,128)} %step.5), channel_id=1, source_target_pairs={{0,32},{32,64},{64,96},{96,128},{128,160},{160,192},{192,224},{256... | collective-permute-start | bytes 147464 | tf_op jit(solution)/shard_map/ppermute | solution.py:245
  63.0 26.6 %collective-permute-start.9 = (f32[96,128]{1,0:T(8,128)}, f32[96,128]{1,0:T(8,128)S(1)}, u32[]{:S(2)}, u32[]{:S(2)}) collective-permute-start(f32[96,128]{1,0:T(8,128)} %step.5), channel_id=1, source_target_pairs={{224,256},{480,0},{225,257},{481,1},{226,258},{482,2},{227,259},{4... | collective-permute-start | bytes 147464 | tf_op jit(solution)/shard_map/ppermute | solution.py:247
  72.6 1.9 %copy-start.4 = (bf16[2,1536,512]{2,1,0:T(8,128)(2,1)S(1)}, bf16[2,1536,512]{2,1,0:T(8,128)(2,1)}, u32[]{:S(2)}) copy-start(bf16[2,1536,512]{2,1,0:T(8,128)(2,1)} %get-tuple-element.8.table_ref) | copy-start | bytes 9437188
  74.5 8.0 %copy-start.5 = (bf16[2,1536,512]{2,1,0:T(8,128)(2,1)S(1)}, bf16[2,1536,512]{2,1,0:T(8,128)(2,1)}, u32[]{:S(2)}) copy-start(bf16[2,1536,512]{2,1,0:T(8,128)(2,1)} %get-tuple-element.8.table_ref) | copy-start | bytes 9437188
  78.0 0.7 copy-start.2
  78.8 0.6 copy-start.15
  81.1 5.7 %copy-start.13 = (f32[96,128]{1,0:T(8,128)S(1)}, f32[96,128]{1,0:T(8,128)}, u32[]{:S(2)}) copy-start(f32[96,128]{1,0:T(8,128)} %step.6) | copy-start | bytes 147460
  81.1 8.6 %collective-permute-start.8 = (f32[96,128]{1,0:T(8,128)}, f32[96,128]{1,0:T(8,128)S(1)}, u32[]{:S(2)}, u32[]{:S(2)}) collective-permute-start(f32[96,128]{1,0:T(8,128)} %step.6), channel_id=1, source_target_pairs={{0,32},{32,64},{64,96},{96,128},{128,160},{160,192},{192,224},{256... | collective-permute-start | bytes 147464 | tf_op jit(solution)/shard_map/ppermute | solution.py:245
  86.0 0.8 copy-start
  86.8 14.7 %collective-permute-start.11 = (f32[96,128]{1,0:T(8,128)S(1)}, f32[96,128]{1,0:T(8,128)S(1)}, u32[]{:S(2)}, u32[]{:S(2)}) collective-permute-start(f32[96,128]{1,0:T(8,128)S(1)} %copy-done.13), channel_id=1, source_target_pairs={{224,256},{480,0},{225,257},{481,1},{226,258},{482,2},{227,259},{4... | collective-permute-start | bytes 147464 | tf_op jit(solution)/shard_map/ppermute | solution.py:247
  90.3 0.6 copy-start.12
  92.8 5.9 %copy-start.8 = (f32[96,128]{1,0:T(8,128)S(1)}, f32[96,128]{1,0:T(8,128)}, u32[]{:S(2)}) copy-start(f32[96,128]{1,0:T(8,128)} %step.7) | copy-start | bytes 147460
  92.8 8.7 %collective-permute-start.10 = (f32[96,128]{1,0:T(8,128)}, f32[96,128]{1,0:T(8,128)S(1)}, u32[]{:S(2)}, u32[]{:S(2)}) collective-permute-start(f32[96,128]{1,0:T(8,128)} %step.7), channel_id=1, source_target_pairs={{0,32},{32,64},{64,96},{96,128},{128,160},{160,192},{192,224},{256... | collective-permute-start | bytes 147464 | tf_op jit(solution)/shard_map/ppermute | solution.py:245
  97.9 0.8 copy-start.1
  98.6 11.3 %collective-permute-start.14 = (f32[96,128]{1,0:T(8,128)S(1)}, f32[96,128]{1,0:T(8,128)S(1)}, u32[]{:S(2)}, u32[]{:S(2)}) collective-permute-start(f32[96,128]{1,0:T(8,128)S(1)} %copy-done.8), channel_id=1, source_target_pairs={{224,256},{480,0},{225,257},{481,1},{226,258},{482,2},{227,259},{4... | collective-permute-start | bytes 147464 | tf_op jit(solution)/shard_map/ppermute | solution.py:247
  102.1 0.6 copy-start.11
  104.6 6.2 %collective-permute-start.13 = (f32[96,128]{1,0:T(8,128)}, f32[96,128]{1,0:T(8,128)S(1)}, u32[]{:S(2)}, u32[]{:S(2)}) collective-permute-start(f32[96,128]{1,0:T(8,128)} %step.8), channel_id=1, source_target_pairs={{0,32},{32,64},{64,96},{96,128},{128,160},{160,192},{192,224},{256... | collective-permute-start | bytes 147464 | tf_op jit(solution)/shard_map/ppermute | solution.py:245
  105.9 8.6 %collective-permute-start.12 = (f32[96,128]{1,0:T(8,128)}, f32[96,128]{1,0:T(8,128)S(1)}, u32[]{:S(2)}, u32[]{:S(2)}) collective-permute-start(f32[96,128]{1,0:T(8,128)} %step.8), channel_id=1, source_target_pairs={{224,256},{480,0},{225,257},{481,1},{226,258},{482,2},{227,259},{4... | collective-permute-start | bytes 147464 | tf_op jit(solution)/shard_map/ppermute | solution.py:247
  110.0 0.8 copy-start.14
  110.8 0.6 copy-start.6
  113.2 6.2 %collective-permute-start.15 = (f32[96,128]{1,0:T(8,128)}, f32[96,128]{1,0:T(8,128)S(1)}, u32[]{:S(2)}, u32[]{:S(2)}) collective-permute-start(f32[96,128]{1,0:T(8,128)} %step.9), channel_id=1, source_target_pairs={{0,32},{32,64},{64,96},{96,128},{128,160},{160,192},{192,224},{256... | collective-permute-start | bytes 147464 | tf_op jit(solution)/shard_map/ppermute | solution.py:245
  (2 other events, 1.2 us)

commit v2 on v1

v2 whole, which is shorter than its diff:
```python
import functools
import math

import jax
import jax.numpy as jnp
from jax import lax
from jax.experimental import pallas as pl
from jax.experimental.pallas import tpu as pltpu
from jax.sharding import PartitionSpec as P

RAYS = 1024
PATCHES = 256
HOPS = 4
TILES = 32
ROWS = 48
CHUNK = 256
GROUPS = RAYS // 128
VMEM = pl.BlockSpec(memory_space=pltpu.VMEM)
SMEM = pl.BlockSpec(memory_space=pltpu.SMEM)
SMALL = pltpu.CompilerParams(vmem_limit_bytes=4 * 1024 * 1024)
LARGE = pltpu.CompilerParams(vmem_limit_bytes=12 * 1024 * 1024)


def partner(axis, mask):
    shift = {"x": 3, "z": 1, "core": 0}[axis]
    return [(s, s ^ (mask << shift)) for s in range(TILES)]


def coefficients_kernel(defl_hbm, shear_hbm, out_ref, defl_ref, shear_ref, defl_sem, shear_sem):
    copies = (
        pltpu.make_async_copy(defl_hbm, defl_ref, defl_sem),
        pltpu.make_async_copy(shear_hbm, shear_ref, shear_sem),
    )
    for copy in copies:
        copy.start()
    for copy in copies:
        copy.wait()
    angle = lax.broadcasted_iota(jnp.int32, (8, PATCHES), 0)
    root = math.sqrt(0.5)
    cos_y, sin_y = jnp.zeros((8, PATCHES), jnp.float32), jnp.zeros((8, PATCHES), jnp.float32)
    for j, (c, s) in enumerate(
        [(1, 0), (root, root), (0, 1), (-root, root), (-1, 0), (-root, -root), (0, -1), (root, -root)]
    ):
        cos_y = jnp.where(angle == j, c, cos_y)
        sin_y = jnp.where(angle == j, s, sin_y)
    for plane in range(2):
        for k in range(5):
            source, first = (defl_ref, k * 32) if k < 2 else (shear_ref, (k - 2) * 32)
            cells = source[0, plane, first : first + 32, :].astype(jnp.float32) * (1.0 / 32.0)
            r0, r1, r2, r3 = [cells[i * 8 : i * 8 + 8] for i in range(4)]
            for a, part in enumerate((r0 + r1 + r2 + r3, r0 - r2, r1 - r3)):
                row = plane * ROWS + k * 9 + a * 3
                out_ref[row : row + 1, :] = jnp.sum(part, axis=0, keepdims=True)
                out_ref[row + 1 : row + 2, :] = jnp.sum(part * cos_y, axis=0, keepdims=True)
                out_ref[row + 2 : row + 3, :] = jnp.sum(part * sin_y, axis=0, keepdims=True)
        out_ref[plane * ROWS + 45 : plane * ROWS + 48, :] = jnp.zeros((3, PATCHES), jnp.float32)


def coefficients(deflection, shear):
    return pl.pallas_call(
        coefficients_kernel,
        out_shape=jax.ShapeDtypeStruct((2 * ROWS, PATCHES), jnp.float32),
        in_specs=[pl.BlockSpec(memory_space=pltpu.HBM)] * 2,
        out_specs=VMEM,
        scratch_shapes=[
            pltpu.VMEM(deflection.shape, deflection.dtype),
            pltpu.VMEM(shear.shape, shear.dtype),
            pltpu.SemaphoreType.DMA,
            pltpu.SemaphoreType.DMA,
        ],
        compiler_params=SMALL,
        name="coefficients",
    )(*[pltpu.with_memory_space_constraint(a, pltpu.HBM) for a in (deflection, shear)])


def join_kernel(count, *refs):
    out_ref, place = refs[-1], 0
    for ref in refs[:count]:
        out_ref[place : place + ref.shape[0]] = ref[...]
        place += ref.shape[0]


def join(blocks, after=()):
    shape = (sum(b.shape[0] for b in blocks), *blocks[0].shape[1:])
    return pl.pallas_call(
        functools.partial(join_kernel, len(blocks)),
        out_shape=jax.ShapeDtypeStruct(shape, blocks[0].dtype),
        in_specs=[VMEM] * (len(blocks) + len(after)),
        out_specs=VMEM,
        compiler_params=SMALL,
        name="join",
    )(*blocks, *after)


def fill_table(sources, table_ref, count):
    place = 0
    for ref in sources:
        for block in range(max(0, ref.shape[0] - count), ref.shape[0]):
            for plane in range(2):
                values = ref[block, plane * ROWS : (plane + 1) * ROWS, :]
                high = values.astype(jnp.bfloat16)
                low = (values - high.astype(jnp.float32)).astype(jnp.bfloat16)
                table_ref[plane, place * ROWS : (place + 1) * ROWS, :PATCHES] = high
                table_ref[plane, place * ROWS : (place + 1) * ROWS, PATCHES:] = low
            place += 1


def find_rows(hop, tiles, table_ref, rel_ref, patch_ref, out_ref, before_ref=None):
    for plane in range(2):
        for chunk in range(RAYS // CHUNK):
            lanes = slice(chunk * CHUNK, (chunk + 1) * CHUNK)
            row = hop * 2 + plane
            patch = patch_ref[row : row + 1, lanes]
            rel = rel_ref[row : row + 1, lanes]
            onehot = lax.broadcasted_iota(jnp.int32, (PATCHES, CHUNK), 0) == patch
            onehot = jnp.where(onehot, 1.0, 0.0).astype(jnp.bfloat16)
            onehot = jnp.concatenate([onehot, onehot], axis=0)
            found = jnp.dot(table_ref[plane, : len(tiles) * ROWS], onehot, preferred_element_type=jnp.float32)
            total = [jnp.zeros((8, CHUNK), jnp.float32) for _ in range(ROWS // 8)]
            wide = jnp.broadcast_to(rel, (8, CHUNK))
            for place, tile in enumerate(tiles):
                here = wide == tile
                for part in range(ROWS // 8):
                    first = place * ROWS + part * 8
                    total[part] = total[part] + jnp.where(here, found[first : first + 8], 0.0)
            for part in range(ROWS // 8):
                for half in range(CHUNK // 128):
                    group = chunk * (CHUNK // 128) + half
                    first = (plane * ROWS + part * 8) * GROUPS + group
                    place = pl.ds(first, 8, stride=GROUPS)
                    sums = total[part][:, half * 128 : half * 128 + 128]
                    out_ref[place, :] = sums if before_ref is None else sums + before_ref[place, :]


def table_kernel(*refs):
    fill_table(refs[:-1], refs[-1], TILES)


def table_of(sources):
    count = sum(source.shape[0] for source in sources)
    return pl.pallas_call(
        table_kernel,
        out_shape=jax.ShapeDtypeStruct((2, count * ROWS, 2 * PATCHES), jnp.bfloat16),
        in_specs=[VMEM] * len(sources),
        out_specs=VMEM,
        compiler_params=LARGE,
        name="table",
    )(*sources)


def lookup_kernel(hops, tiles, count, blocks, added, *refs):
    sources, (rel_ref, patch_ref), refs = refs[:count], refs[count : count + 2], refs[count + 2 :]
    before = refs[: len(hops)] if added else [None] * len(hops)
    outs = refs[-len(hops) :]
    if blocks:
        *outs, table_ref = refs[-1 - len(hops) :]
        fill_table(sources, table_ref, blocks)
    else:
        (table_ref,) = sources
    for hop, before_ref, out_ref in zip(hops, before, outs, strict=True):
        find_rows(hop, tiles, table_ref, rel_ref, patch_ref, out_ref, before_ref)


FOUND = jax.ShapeDtypeStruct((2 * ROWS * GROUPS, 128), jnp.float32)


COSTLY = pl.CostEstimate(flops=4000000000, bytes_accessed=100000, transcendentals=0)
COSTLIER = pl.CostEstimate(flops=16000000000, bytes_accessed=100000, transcendentals=0)
COST = pl.CostEstimate(flops=100000, bytes_accessed=100000, transcendentals=0)


def scratch_table(tiles):
    return pltpu.VMEM((2, len(tiles) * ROWS, 2 * PATCHES), jnp.bfloat16)


def lookup(hops, tiles, sources, rel, patch, before=(), blocks=TILES):
    first = len(sources) + 2
    return pl.pallas_call(
        functools.partial(lookup_kernel, hops, tiles, len(sources), blocks, bool(before)),
        out_shape=[FOUND] * len(hops),
        in_specs=[VMEM] * (first + len(before)),
        out_specs=[VMEM] * len(hops),
        input_output_aliases={first + i: i for i in range(len(before))},
        scratch_shapes=[scratch_table(tiles)] if blocks else [],
        compiler_params=LARGE,
        cost_estimate=COSTLIER if blocks else COST if hops[0] == 1 else COST,
        name="lookup",
    )(*sources, rel, patch, *before)


def sine(turn):
    v = turn * (2.0 * math.pi)
    v2 = v * v
    poly = 1.0 / 6227020800.0
    for c in (-1.0 / 39916800.0, 1.0 / 362880.0, -1.0 / 5040.0, 1.0 / 120.0, -1.0 / 6.0):
        poly = poly * v2 + c
    return v + v * v2 * poly


def wave(turns):
    t = turns - jnp.floor(turns + 0.5)
    size = jnp.abs(t)
    fold = jnp.where(t >= 0, 0.5 - t, -0.5 - t)
    return sine(0.25 - size), sine(jnp.where(size > 0.25, fold, t))


def advance(state, read):
    pos_x, pos_y, ang_x, ang_y, a11, a12, a21, a22, b11, b12, b21, b22 = state
    cos_x, sin_x = wave(pos_x * 0.25)
    cos_y, sin_y = wave(pos_y * 0.125)
    values = []
    for k in range(5):
        parts = []
        for a in range(3):
            m = [read(k * 9 + a * 3 + b) for b in range(3)]
            parts.append(m[0] + m[1] * cos_y + m[2] * sin_y)
        values.append(parts[0] + parts[1] * cos_x + parts[2] * sin_x)
    alpha_x, alpha_y, psi11, psi12, psi22 = values
    ang_x = ang_x - alpha_x
    ang_y = ang_y - alpha_y
    b11 = b11 - (psi11 * a11 + psi12 * a21)
    b12 = b12 - (psi11 * a12 + psi12 * a22)
    b21 = b21 - (psi12 * a11 + psi22 * a21)
    b22 = b22 - (psi12 * a12 + psi22 * a22)
    pos_x = pos_x + 0.5 * ang_x
    pos_y = pos_y + 0.5 * ang_y
    a11 = a11 + 0.5 * b11
    a12 = a12 + 0.5 * b12
    a21 = a21 + 0.5 * b21
    a22 = a22 + 0.5 * b22
    return [pos_x, pos_y, ang_x, ang_y, a11, a12, a21, a22, b11, b12, b21, b22]


def rows(ref, k):
    return ref[k * GROUPS : (k + 1) * GROUPS, :]


def both_planes(state, read):
    for plane in range(2):
        state = advance(state, lambda k, plane=plane: read(plane * ROWS + k))
    return state


def summed(refs, k):
    return functools.reduce(jnp.add, [rows(ref, k) for ref in refs])


def first_step_kernel(tiles, parts, table_ref, rel_ref, patch_ref, state_ref, *refs):
    part_refs, (out_ref, leaving_ref, found_ref) = refs[:parts], refs[-3:]
    find_rows(0, tiles, table_ref, rel_ref, patch_ref, found_ref)
    found = (*part_refs, found_ref)
    state = both_planes([rows(state_ref, k) for k in range(12)], lambda k: summed(found, k))
    for k in range(12):
        out_ref[k * GROUPS : (k + 1) * GROUPS, :] = state[k]
        leaving_ref[k * GROUPS : (k + 1) * GROUPS, :] = state[k]


MOVED = jax.ShapeDtypeStruct((12 * GROUPS, 128), jnp.float32)
CROSSING = (100,108,108,204)


def moved_out(senders, step):
    return jax.ShapeDtypeStruct((CROSSING[step], 128), jnp.float32) if senders else MOVED


def first_step(tiles, table, rel, patch, state, parts):
    return pl.pallas_call(
        functools.partial(first_step_kernel, tiles, len(parts)),
        out_shape=[MOVED, moved_out(True, 0)],
        in_specs=[VMEM] * (4 + len(parts)),
        out_specs=[VMEM] * 2,
        scratch_shapes=[pltpu.VMEM(FOUND.shape, FOUND.dtype)],
        compiler_params=LARGE,
        cost_estimate=COST,
        name="first_step",
    )(table, rel, patch, state, *parts)


def step_kernel(senders, step, counts, q_ref, *refs):
    out_ref = refs[-1]
    main_ref, *refs = refs[: sum(counts)]
    wrap_ref = refs.pop(0) if counts[1] else None
    early, late = refs[: counts[2]], refs[counts[2] :]
    q = q_ref[0]
    shape = (GROUPS, 128)

    @pl.when((q == RUN - 1) == senders)
    def _():
        behind = jnp.full(shape, q, jnp.int32) < step
        crossed = jnp.full(shape, q, jnp.int32) == 0
        state = [rows(main_ref, k) for k in range(12)]
        if wrap_ref is not None and step > 1:
            state = [jnp.where(crossed, rows(wrap_ref, k), state[k]) for k in range(12)]

        def read(k):
            if not early:
                return summed(late, k)
            if not late:
                return summed(early, k)
            return jnp.where(behind, summed(late, k), summed(early, k))

        state = both_planes(state, read)
        if wrap_ref is not None and step == 1:
            state = [jnp.where(crossed, rows(wrap_ref, k), state[k]) for k in range(12)]
        for k in range(12):
            out_ref[k * GROUPS : (k + 1) * GROUPS, :] = state[k]


def run_step(senders, step, q, main, wrap, found, after=()):
    crossed = [] if senders else [wrap]
    early = found[step : step + 1]
    late = found[step - 1 : step] if step >= 2 and not senders else []
    args = [main, *crossed, *early, *late]
    return pl.pallas_call(
        functools.partial(step_kernel, senders, step, (1, len(crossed), len(early), len(late))),
        out_shape=moved_out(senders, step),
        in_specs=[SMEM] + [VMEM] * (len(args) + len(after)),
        out_specs=VMEM,
        compiler_params=SMALL,
        cost_estimate=COST,
        name="step",
    )(q, *args, *after)


RUN = 8


def tiles_of(masks, core):
    return tuple(m * 8 + j * 2 + core for m in masks for j in range(4))


def mixed(axis_first, axis_second):
    pairs = []
    for s in range(TILES):
        mask = axis_first if s % 2 == 0 else axis_second
        pairs.append((s, s ^ (mask << 3)))
    return pairs


def body(state, deflection, shear, routes, patches):
    slabs = lax.axis_size("los")
    slab = lax.axis_index("los")
    q = (slab % RUN).astype(jnp.int32).reshape(1)
    across = [(i, (i + 1) % slabs) for i in range(slabs) if i % RUN == RUN - 1]

    def onward(step):
        idle = {step} if step < HOPS else set(range(HOPS, RUN))
        return [(i, i + 1) for i in range(slabs) if i % RUN != RUN - 1 and i % RUN not in idle]

    route, patch = routes.reshape(2 * HOPS, RAYS), patches.reshape(2 * HOPS, RAYS)
    rel = jnp.bitwise_xor(route, lax.axis_index("sky").astype(jnp.int32))
    rel = jnp.bitwise_xor(rel, ((rel >> 3) & route & 1) << 4)
    rays = state.reshape(12 * GROUPS, 128)

    own = coefficients(deflection, shear)
    column = [own] + [lax.ppermute(own, "sky", partner("z", m)) for m in (1, 2, 3)]
    column = join([block[None] for block in column], [rel, patch, rays])
    near = [lax.ppermute(column, "sky", mixed(1, 3)), lax.ppermute(column, "sky", mixed(3, 1))]
    far = lax.ppermute(column, "sky", partner("x", 2))

    hops = range(HOPS)
    chip = partner("core", 1)
    found = lookup(hops, tiles_of((0, 1), 0), [column, near[0]], rel, patch)
    found = lookup(hops, tiles_of((3,), 0), [near[1]], rel, patch, found)
    other = [lax.ppermute(join([column, *near], found), "sky", chip), lax.ppermute(far, "sky", chip)]
    found = list(lookup([0], tiles_of((2,), 0), [far], rel, patch, found[:1])) + list(found[1:])
    there = tiles_of((0, 1, 3, 2), 1)
    other = table_of([*other, far])
    moved, leaving = first_step(there, other, rel, patch, rays, found[:1])
    wraps, kept = [lax.ppermute(leaving, "los", across)], moved
    main, before = lax.ppermute(moved, "los", onward(0)), None
    for step in range(1, HOPS + 1):
        if step < HOPS:
            (found[step],) = lookup([step], there + tiles_of((2,), 0), [other], rel, patch, found[step : step + 1], 0)
        after = ()
        if step < HOPS:
            leaving = run_step(True, step, q, main, None, found)
            wraps.append(lax.ppermute(leaving, "los", across))
            after = (leaving,)
        moved = run_step(False, step, q, main, wraps[step - 2] if step >= 2 else kept, found, after)
        main, before = lax.ppermute(moved, "los", onward(step)), main
    out = jnp.where(q[0] == 0, wraps[HOPS - 1][:96], jnp.where(q[0] <= HOPS, main, before))
    return out.reshape(12, RAYS)


def solution(mesh):
    placed = (
        P(None, ("los", "sky")),
        P("los", None, None, "sky"),
        P("los", None, None, "sky"),
        P(None, None, ("los", "sky"), None),
        P(None, None, ("los", "sky")),
    )
    return jax.shard_map(
        body, mesh=mesh, in_specs=placed, out_specs=P(None, ("los", "sky")), check_vma=False
    )
```

time: 122 us -> 86.1 us (0.71)
  waiting for transfers between devices: 31.1 us -> 14 us
  local copies, waits for them, and re-layouts: 10.9 us -> 2.3 us
  Pallas kernels: 25.6 us -> 18.8 us
  starting transfers between devices: 51 us -> 48.2 us
    ppermute x16 -> x17, waiting for transfers between devices: 31.1 us -> 14 us  [the longest x4 4.71 us: body(): main, before = (lax.ppermute(moved, 'los', onward(step)), main)]
    unnamed x42 -> x0, local copies, waits for them, and re-layouts: 9.56 us -> none
    pallas_call x9 -> x17, Pallas kernels: 23.8 us -> 17.6 us  [the longest x6 15.1 us: lookup(): pl.pallas_call(functools.partial(lookup_kernel, hops, tiles, len(sources)...]
    ppermute x16 -> x17, starting transfers between devices: 51 us -> 48.2 us  [the longest x3 12.3 us: body(): lax.ppermute(own, 'sky', partner('z', m))]
  transfers between devices with their start and end apart: 16 -> 17, of which waited for: 8 -> 6; matrix products, arithmetic and copies ran while one was open for 1% -> 3% of each run, Pallas kernels for 15% -> 18%
where the time goes in v2:
time: 86.1 us; the launch traced here: 84.4 us
  starting transfers between devices  48.2 us (56%)
  Pallas kernels  18.8 us (22%)
  waiting for transfers between devices  14 us (16%)
  local copies, waits for them, and re-layouts  2.3 us (3%)
  other arithmetic  0.88 us (1%)
    pallas_call x6, Pallas kernels, lookup(): pl.pallas_call(functools.partial(lookup_kernel, hops, tiles, len(sources)...  15.1 us
    ppermute x3, starting transfers between devices, body(): lax.ppermute(own, 'sky', partner('z', m))  12.3 us
    ppermute x3, starting transfers between devices, body(): wraps.append(lax.ppermute(leaving, 'los', across))  9.28 us
    ppermute x1, starting transfers between devices, body(): wraps, kept = ([lax.ppermute(leaving, 'los', across)], moved)  6.97 us
    ppermute x4, waiting for transfers between devices, body(): main, before = (lax.ppermute(moved, 'los', onward(step)), main)  4.71 us
    ppermute x4, starting transfers between devices, body(): main, before = (lax.ppermute(moved, 'los', onward(step)), main)  4.53 us
    ppermute x1, starting transfers between devices, body(): lax.ppermute(column, 'sky', mixed(3, 1))  4 us
    ppermute x3, waiting for transfers between devices, body(): lax.ppermute(own, 'sky', partner('z', m))  3.92 us
  transfers between devices with their start and end apart: 17, of which 6 were waited for; matrix products, arithmetic and copies ran while one was open for 3% of the time, Pallas kernels for 18%

profile of v2, /device:TPU:56, one launch (start us, length us, event | category | flops | bytes accessed | tf_op | source)
XLA Modules:
  0.0 84.4 jit_solution(17640083738706251019)
XLA Ops:
  0.0 1.2 %coefficients.1 = f32[96,256]{1,0:T(8,128)S(1)} custom-call(bf16[1,2,64,256]{3,2,1,0:T(8,128)(2,1)} %defl_hbm.1, bf16[1,2,96,256]{3,2,1,0:T(8,128)(2,1)} %shear_hbm.1), custom_call_target="tpu_custom_call" | custom-call | tf_op jit(solution)/shard_map/coefficients/pallas_call | solution.py:60
  1.2 4.3 %collective-permute-start = (f32[96,256]{1,0:T(8,128)S(1)}, f32[96,256]{1,0:T(8,128)S(1)}, u32[]{:S(2)}, u32[]{:S(2)}) collective-permute-start(f32[96,256]{1,0:T(8,128)S(1)} %coefficients.1), channel_id=1, source_target_pairs={{0,2},{1,3},{2,0},{3,1},{4,6},{5,7},{6,4},{7,5},{8,10},{9,11},{10,... | collective-permute-start | bytes 294920 | tf_op jit(solution)/shard_map/ppermute | solution.py:356
  5.5 6.1 %collective-permute-start.1 = (f32[96,256]{1,0:T(8,128)S(1)}, f32[96,256]{1,0:T(8,128)S(1)}, u32[]{:S(2)}, u32[]{:S(2)}) collective-permute-start(f32[96,256]{1,0:T(8,128)S(1)} %coefficients.1), channel_id=1, source_target_pairs={{0,4},{1,5},{2,6},{3,7},{4,0},{5,1},{6,2},{7,3},{8,12},{9,13},{10,... | collective-permute-start | bytes 294920 | tf_op jit(solution)/shard_map/ppermute | solution.py:356
  11.6 1.9 %collective-permute-start.2 = (f32[96,256]{1,0:T(8,128)S(1)}, f32[96,256]{1,0:T(8,128)S(1)}, u32[]{:S(2)}, u32[]{:S(2)}) collective-permute-start(f32[96,256]{1,0:T(8,128)S(1)} %coefficients.1), channel_id=1, source_target_pairs={{0,6},{1,7},{2,4},{3,5},{4,2},{5,3},{6,0},{7,1},{8,14},{9,15},{10,... | collective-permute-start | bytes 294920 | tf_op jit(solution)/shard_map/ppermute | solution.py:356
  13.5 0.9 %reduce = s32[4,2,1024]{2,1,0:T(2,128)S(1)} reduce(s32[4,2,1024,1]{2,3,1,0:T(1,128)} %param.8, s32[]{:T(128)} %constant.23.clone.1), dimensions={3}, to_apply=%param.8.reduce_sub_computation | reduce | bytes 65540 | tf_op args[3]
  14.4 0.8 reshape.17.refs_5_.refs_3_.refs_2_.patch_ref
  15.2 0.9 %reshape.18.refs_6_.state_ref = f32[96,128]{1,0:T(8,128)S(1)} reshape(f32[12,1024]{1,0:T(8,128)} %param.5) | data formatting | bytes 98304 | tf_op jit(solution)/shard_map/reshape | solution.py:353
  16.2 3.8 %collective-permute-done.2 = f32[96,256]{1,0:T(8,128)S(1)} collective-permute-done((f32[96,256]{1,0:T(8,128)S(1)}, f32[96,256]{1,0:T(8,128)S(1)}, u32[]{:S(2)}, u32[]{:S(2)}) %collective-permute-start.2) | collective-permute-done | bytes 98336 | tf_op jit(solution)/shard_map/ppermute | solution.py:356
  20.0 3.4 %collective-permute-start.3 = (f32[4,96,256]{2,1,0:T(8,128)S(1)}, f32[4,96,256]{2,1,0:T(8,128)S(1)}, u32[]{:S(2)}, u32[]{:S(2)}) collective-permute-start(f32[4,96,256]{2,1,0:T(8,128)S(1)} %join.2.refs_0_), channel_id=1, source_target_pairs={{0,8},{1,25},{2,10},{3,27},{4,12},{5,29},{6,14},{7,31},{8,0},{9,17... | collective-permute-start | bytes 1179656 | tf_op jit(solution)/shard_map/ppermute | solution.py:358
  23.4 4.0 %collective-permute-start.4 = (f32[4,96,256]{2,1,0:T(8,128)S(1)}, f32[4,96,256]{2,1,0:T(8,128)S(1)}, u32[]{:S(2)}, u32[]{:S(2)}) collective-permute-start(f32[4,96,256]{2,1,0:T(8,128)S(1)} %join.2.refs_0_), channel_id=1, source_target_pairs={{0,24},{1,9},{2,26},{3,11},{4,28},{5,13},{6,30},{7,15},{8,16},{9,1... | collective-permute-start | bytes 1179656 | tf_op jit(solution)/shard_map/ppermute | solution.py:358
  27.4 2.6 %collective-permute-start.6 = (f32[4,96,256]{2,1,0:T(8,128)S(1)}, f32[4,96,256]{2,1,0:T(8,128)S(1)}, u32[]{:S(2)}, u32[]{:S(2)}) collective-permute-start(f32[4,96,256]{2,1,0:T(8,128)S(1)} %join.2.refs_0_), channel_id=1, source_target_pairs={{0,16},{1,17},{2,18},{3,19},{4,20},{5,21},{6,22},{7,23},{8,24},{9,... | collective-permute-start | bytes 1179656 | tf_op jit(solution)/shard_map/ppermute | solution.py:359
  30.0 2.7 %collective-permute-done.3.refs_1_ = f32[4,96,256]{2,1,0:T(8,128)S(1)} collective-permute-done((f32[4,96,256]{2,1,0:T(8,128)S(1)}, f32[4,96,256]{2,1,0:T(8,128)S(1)}, u32[]{:S(2)}, u32[]{:S(2)}) %collective-permute-start.3) | collective-permute-done | bytes 393248 | tf_op jit(solution)/shard_map/ppermute | solution.py:358
  32.7 4.2 %lookup.6 = (f32[768,128]{1,0:T(8,128)S(1)}, f32[768,128]{1,0:T(8,128)S(1)}, f32[768,128]{1,0:T(8,128)S(1)}, f32[768,128]{1,0:T(8,128)S(1)}) custom-call(f32[4,96,256]{2,1,0:T(8,128)S(1)} %join.2.refs_0_, f32[4,96,256]{2,1,0:T(8,128)S(1)} %collective-permute-done.3.refs_1_, s32[8,1024]{1,0:T(8,128)S(1)} %shift-left_xor_fusion.refs_4_.refs_2_.refs_1_.rel_ref, ...), custom_call_target="tpu_custom_call" | custom-call | flops 16000000000 | bytes 100000 | tf_op jit(solution)/shard_map/lookup/pallas_call | solution.py:178
  36.8 3.1 %lookup.7 = (f32[768,128]{1,0:T(8,128)S(1)}, f32[768,128]{1,0:T(8,128)S(1)}, f32[768,128]{1,0:T(8,128)S(1)}, f32[768,128]{1,0:T(8,128)S(1)}) custom-call(f32[4,96,256]{2,1,0:T(8,128)S(1)} %collective-permute-done.4.refs_0_.refs_2_, ...), custom_call_target="tpu_custom_call", output_to_operand_aliasing={{0}: (3, {}), {1}: (4, {}), {2}: (5, {}), {3}: (6, {})} | custom-call | flops 16000000000 | bytes 100000 | tf_op jit(solution)/shard_map/lookup/pallas_call | solution.py:178
  40.1 1.9 %collective-permute-start.5 = (f32[12,96,256]{2,1,0:T(8,128)S(1)}, f32[12,96,256]{2,1,0:T(8,128)S(1)}, u32[]{:S(2)}, u32[]{:S(2)}) collective-permute-start(f32[12,96,256]{2,1,0:T(8,128)S(1)} %join.3), channel_id=1, source_target_pairs={{0,1},{1,0},{2,3},{3,2},{4,5},{5,4},{6,7},{7,6},{8,9},{9,8},{10,11... | collective-permute-start | bytes 3538952 | tf_op jit(solution)/shard_map/ppermute | solution.py:365
  42.0 1.8 %collective-permute-done.6.refs_2_.refs_0_ = f32[4,96,256]{2,1,0:T(8,128)S(1)} collective-permute-done((f32[4,96,256]{2,1,0:T(8,128)S(1)}, f32[4,96,256]{2,1,0:T(8,128)S(1)}, u32[]{:S(2)}, u32[]{:S(2)}) %collective-permute-start.6) | collective-permute-done | bytes 393248 | tf_op jit(solution)/shard_map/ppermute | solution.py:359
  43.8 1.9 %collective-permute-start.7 = (f32[4,96,256]{2,1,0:T(8,128)S(1)}, f32[4,96,256]{2,1,0:T(8,128)S(1)}, u32[]{:S(2)}, u32[]{:S(2)}) collective-permute-start(f32[4,96,256]{2,1,0:T(8,128)S(1)} %collective-permute-done.6.refs_2_.refs_0_), channel_id=1, source_target_pairs={{0,1},{1,0},{2,3},{3,2},{4,5},{5,4},{6,7},{7,6},{8,9},{9,8},{10,11... | collective-permute-start | bytes 1179656 | tf_op jit(solution)/shard_map/ppermute | solution.py:365
  45.7 0.9 %lookup.8.refs_0_ = f32[768,128]{1,0:T(8,128)S(1)} custom-call(f32[4,96,256]{2,1,0:T(8,128)S(1)} %collective-permute-done.6.refs_2_.refs_0_, s32[8,1024]{1,0:T(8,128)S(1)} %shift-left_xor_fusion.refs_4_.refs_2_.refs_1_.rel_ref, s32[8,1024]{1,0:T(8,128)S(1)} %reshape.17.refs_5_.refs_3_.refs_2_.patch_ref, ...), custom_call_target="tpu_custom_call", output_to_operand_aliasing={{}: (3, {})} | custom-call | flops 16000000000 | bytes 100000 | tf_op jit(solution)/shard_map/lookup/pallas_call | solution.py:178
  46.6 0.8 collective-permute-done.7.refs_1_
  47.7 1.9 %first_step.1 = (f32[96,128]{1,0:T(8,128)S(1)}, f32[100,128]{1,0:T(8,128)S(1)}) custom-call(bf16[2,960,512]{2,1,0:T(8,128)(2,1)S(1)} %table.1.table_ref.refs_0_, s32[8,1024]{1,0:T(8,128)S(1)} %shift-left_xor_fusion.refs_4_.refs_2_.refs_1_.rel_ref, s32[8,1024]{1,0:T(8,128)S(1)} %reshape.17.refs_5_.refs_3_.refs_2_.patch_ref, ...), custom_call_target="tpu_custom_call" | custom-call | flops 100000 | bytes 100000 | tf_op jit(solution)/shard_map/first_step/pallas_call | solution.py:267
  49.5 1.3 %collective-permute-start.8 = (f32[96,128]{1,0:T(8,128)S(1)}, f32[96,128]{1,0:T(8,128)S(1)}, u32[]{:S(2)}, u32[]{:S(2)}) collective-permute-start(f32[96,128]{1,0:T(8,128)S(1)} %get-tuple-element.23.refs_1_), channel_id=1, source_target_pairs={{32,64},{64,96},{96,128},{128,160},{160,192},{192,224},{288,320},{... | collective-permute-start | bytes 147464 | tf_op jit(solution)/shard_map/ppermute | solution.py:371
  50.8 7.0 %collective-permute-start.10 = (f32[100,128]{1,0:T(8,128)S(1)}, f32[100,128]{1,0:T(8,128)S(1)}, u32[]{:S(2)}, u32[]{:S(2)}) collective-permute-start(f32[100,128]{1,0:T(8,128)S(1)} %get-tuple-element.24), channel_id=1, source_target_pairs={{224,256},{480,0},{225,257},{481,1},{226,258},{482,2},{227,259},{4... | collective-permute-start | bytes 153608 | tf_op jit(solution)/shard_map/ppermute | solution.py:370
  57.8 2.3 %lookup.9.refs_1_.refs_2_.refs_3_ = f32[768,128]{1,0:T(8,128)S(1)} custom-call(bf16[2,960,512]{2,1,0:T(8,128)(2,1)S(1)} %table.1.table_ref.refs_0_, s32[8,1024]{1,0:T(8,128)S(1)} %shift-left_xor_fusion.refs_4_.refs_2_.refs_1_.rel_ref, s32[8,1024]{1,0:T(8,128)S(1)} %reshape.17.refs_5_.refs_3_.refs_2_.patch_ref, ...), custom_call_target="tpu_custom_call", output_to_operand_aliasing={{}: (3, {})} | custom-call | flops 100000 | bytes 100000 | tf_op jit(solution)/shard_map/lookup/pallas_call | solution.py:178
  60.3 1.3 %collective-permute-start.9 = (f32[96,128]{1,0:T(8,128)S(1)}, f32[96,128]{1,0:T(8,128)S(1)}, u32[]{:S(2)}, u32[]{:S(2)}) collective-permute-start(f32[96,128]{1,0:T(8,128)S(1)} %step.8), channel_id=1, source_target_pairs={{0,32},{64,96},{96,128},{128,160},{160,192},{192,224},{256,288},{3... | collective-permute-start | bytes 147464 | tf_op jit(solution)/shard_map/ppermute | solution.py:381
  61.6 2.3 %lookup.10.refs_1_.refs_2_.refs_3_ = f32[768,128]{1,0:T(8,128)S(1)} custom-call(bf16[2,960,512]{2,1,0:T(8,128)(2,1)S(1)} %table.1.table_ref.refs_0_, s32[8,1024]{1,0:T(8,128)S(1)} %shift-left_xor_fusion.refs_4_.refs_2_.refs_1_.rel_ref, s32[8,1024]{1,0:T(8,128)S(1)} %reshape.17.refs_5_.refs_3_.refs_2_.patch_ref, ...), custom_call_target="tpu_custom_call", output_to_operand_aliasing={{}: (3, {})} | custom-call | flops 100000 | bytes 100000 | tf_op jit(solution)/shard_map/lookup/pallas_call | solution.py:178
  63.9 5.7 %collective-permute-start.13 = (f32[108,128]{1,0:T(8,128)S(1)}, f32[108,128]{1,0:T(8,128)S(1)}, u32[]{:S(2)}, u32[]{:S(2)}) collective-permute-start(f32[108,128]{1,0:T(8,128)S(1)} %step.7.refs_3_), channel_id=1, source_target_pairs={{224,256},{480,0},{225,257},{481,1},{226,258},{482,2},{227,259},{4... | collective-permute-start | bytes 165896 | tf_op jit(solution)/shard_map/ppermute | solution.py:378
  69.7 1.3 %collective-permute-start.11 = (f32[96,128]{1,0:T(8,128)S(1)}, f32[96,128]{1,0:T(8,128)S(1)}, u32[]{:S(2)}, u32[]{:S(2)}) collective-permute-start(f32[96,128]{1,0:T(8,128)S(1)} %step.10), channel_id=1, source_target_pairs={{0,32},{32,64},{96,128},{128,160},{160,192},{192,224},{256,288},{2... | collective-permute-start | bytes 147464 | tf_op jit(solution)/shard_map/ppermute | solution.py:381
  71.0 2.3 %collective-permute-start.15 = (f32[108,128]{1,0:T(8,128)S(1)}, f32[108,128]{1,0:T(8,128)S(1)}, u32[]{:S(2)}, u32[]{:S(2)}) collective-permute-start(f32[108,128]{1,0:T(8,128)S(1)} %step.9.refs_4_), channel_id=1, source_target_pairs={{224,256},{480,0},{225,257},{481,1},{226,258},{482,2},{227,259},{4... | collective-permute-start | bytes 165896 | tf_op jit(solution)/shard_map/ppermute | solution.py:378
  73.3 2.3 %lookup.11.refs_1_.refs_2_ = f32[768,128]{1,0:T(8,128)S(1)} custom-call(bf16[2,960,512]{2,1,0:T(8,128)(2,1)S(1)} %table.1.table_ref.refs_0_, s32[8,1024]{1,0:T(8,128)S(1)} %shift-left_xor_fusion.refs_4_.refs_2_.refs_1_.rel_ref, s32[8,1024]{1,0:T(8,128)S(1)} %reshape.17.refs_5_.refs_3_.refs_2_.patch_ref, ...), custom_call_target="tpu_custom_call", output_to_operand_aliasing={{}: (3, {})} | custom-call | flops 100000 | bytes 100000 | tf_op jit(solution)/shard_map/lookup/pallas_call | solution.py:178
  75.8 1.3 %collective-permute-start.12 = (f32[204,128]{1,0:T(8,128)S(1)}, f32[204,128]{1,0:T(8,128)S(1)}, u32[]{:S(2)}, u32[]{:S(2)}) collective-permute-start(f32[204,128]{1,0:T(8,128)S(1)} %step.11.refs_4_), channel_id=1, source_target_pairs={{224,256},{480,0},{225,257},{481,1},{226,258},{482,2},{227,259},{4... | collective-permute-start | bytes 313352 | tf_op jit(solution)/shard_map/ppermute | solution.py:378
  77.1 1.3 %collective-permute-start.14 = (f32[96,128]{1,0:T(8,128)S(1)}, f32[96,128]{1,0:T(8,128)S(1)}, u32[]{:S(2)}, u32[]{:S(2)}) collective-permute-start(f32[96,128]{1,0:T(8,128)S(1)} %step.12), channel_id=1, source_target_pairs={{0,32},{32,64},{64,96},{128,160},{160,192},{192,224},{256,288},{28... | collective-permute-start | bytes 147464 | tf_op jit(solution)/shard_map/ppermute | solution.py:381
  78.4 4.7 %collective-permute-done.14.refs_0_ = f32[96,128]{1,0:T(8,128)S(1)} collective-permute-done((f32[96,128]{1,0:T(8,128)S(1)}, f32[96,128]{1,0:T(8,128)S(1)}, u32[]{:S(2)}, u32[]{:S(2)}) %collective-permute-start.14) | collective-permute-done | bytes 49184 | tf_op jit(solution)/shard_map/ppermute | solution.py:381
  (27 shorter events, 2.1 us)
Async XLA Ops:
  1.2 14.9 %collective-permute-start = (f32[96,256]{1,0:T(8,128)S(1)}, f32[96,256]{1,0:T(8,128)S(1)}, u32[]{:S(2)}, u32[]{:S(2)}) collective-permute-start(f32[96,256]{1,0:T(8,128)S(1)} %coefficients.1), channel_id=1, source_target_pairs={{0,2},{1,3},{2,0},{3,1},{4,6},{5,7},{6,4},{7,5},{8,10},{9,11},{10,... | collective-permute-start | bytes 294920 | tf_op jit(solution)/shard_map/ppermute | solution.py:356
  5.5 10.7 %collective-permute-start.1 = (f32[96,256]{1,0:T(8,128)S(1)}, f32[96,256]{1,0:T(8,128)S(1)}, u32[]{:S(2)}, u32[]{:S(2)}) collective-permute-start(f32[96,256]{1,0:T(8,128)S(1)} %coefficients.1), channel_id=1, source_target_pairs={{0,4},{1,5},{2,6},{3,7},{4,0},{5,1},{6,2},{7,3},{8,12},{9,13},{10,... | collective-permute-start | bytes 294920 | tf_op jit(solution)/shard_map/ppermute | solution.py:356
  11.6 8.4 %collective-permute-start.2 = (f32[96,256]{1,0:T(8,128)S(1)}, f32[96,256]{1,0:T(8,128)S(1)}, u32[]{:S(2)}, u32[]{:S(2)}) collective-permute-start(f32[96,256]{1,0:T(8,128)S(1)} %coefficients.1), channel_id=1, source_target_pairs={{0,6},{1,7},{2,4},{3,5},{4,2},{5,3},{6,0},{7,1},{8,14},{9,15},{10,... | collective-permute-start | bytes 294920 | tf_op jit(solution)/shard_map/ppermute | solution.py:356
  20.0 12.6 %collective-permute-start.3 = (f32[4,96,256]{2,1,0:T(8,128)S(1)}, f32[4,96,256]{2,1,0:T(8,128)S(1)}, u32[]{:S(2)}, u32[]{:S(2)}) collective-permute-start(f32[4,96,256]{2,1,0:T(8,128)S(1)} %join.2.refs_0_), channel_id=1, source_target_pairs={{0,8},{1,25},{2,10},{3,27},{4,12},{5,29},{6,14},{7,31},{8,0},{9,17... | collective-permute-start | bytes 1179656 | tf_op jit(solution)/shard_map/ppermute | solution.py:358
  23.4 13.4 %collective-permute-start.4 = (f32[4,96,256]{2,1,0:T(8,128)S(1)}, f32[4,96,256]{2,1,0:T(8,128)S(1)}, u32[]{:S(2)}, u32[]{:S(2)}) collective-permute-start(f32[4,96,256]{2,1,0:T(8,128)S(1)} %join.2.refs_0_), channel_id=1, source_target_pairs={{0,24},{1,9},{2,26},{3,11},{4,28},{5,13},{6,30},{7,15},{8,16},{9,1... | collective-permute-start | bytes 1179656 | tf_op jit(solution)/shard_map/ppermute | solution.py:358
  27.4 16.4 %collective-permute-start.6 = (f32[4,96,256]{2,1,0:T(8,128)S(1)}, f32[4,96,256]{2,1,0:T(8,128)S(1)}, u32[]{:S(2)}, u32[]{:S(2)}) collective-permute-start(f32[4,96,256]{2,1,0:T(8,128)S(1)} %join.2.refs_0_), channel_id=1, source_target_pairs={{0,16},{1,17},{2,18},{3,19},{4,20},{5,21},{6,22},{7,23},{8,24},{9,... | collective-permute-start | bytes 1179656 | tf_op jit(solution)/shard_map/ppermute | solution.py:359
  40.1 7.4 %collective-permute-start.5 = (f32[12,96,256]{2,1,0:T(8,128)S(1)}, f32[12,96,256]{2,1,0:T(8,128)S(1)}, u32[]{:S(2)}, u32[]{:S(2)}) collective-permute-start(f32[12,96,256]{2,1,0:T(8,128)S(1)} %join.3), channel_id=1, source_target_pairs={{0,1},{1,0},{2,3},{3,2},{4,5},{5,4},{6,7},{7,6},{8,9},{9,8},{10,11... | collective-permute-start | bytes 3538952 | tf_op jit(solution)/shard_map/ppermute | solution.py:365
  43.8 3.6 %collective-permute-start.7 = (f32[4,96,256]{2,1,0:T(8,128)S(1)}, f32[4,96,256]{2,1,0:T(8,128)S(1)}, u32[]{:S(2)}, u32[]{:S(2)}) collective-permute-start(f32[4,96,256]{2,1,0:T(8,128)S(1)} %collective-permute-done.6.refs_2_.refs_0_), channel_id=1, source_target_pairs={{0,1},{1,0},{2,3},{3,2},{4,5},{5,4},{6,7},{7,6},{8,9},{9,8},{10,11... | collective-permute-start | bytes 1179656 | tf_op jit(solution)/shard_map/ppermute | solution.py:365
  49.5 10.6 %collective-permute-start.8 = (f32[96,128]{1,0:T(8,128)S(1)}, f32[96,128]{1,0:T(8,128)S(1)}, u32[]{:S(2)}, u32[]{:S(2)}) collective-permute-start(f32[96,128]{1,0:T(8,128)S(1)} %get-tuple-element.23.refs_1_), channel_id=1, source_target_pairs={{32,64},{64,96},{96,128},{128,160},{160,192},{192,224},{288,320},{... | collective-permute-start | bytes 147464 | tf_op jit(solution)/shard_map/ppermute | solution.py:371
  50.8 18.9 %collective-permute-start.10 = (f32[100,128]{1,0:T(8,128)S(1)}, f32[100,128]{1,0:T(8,128)S(1)}, u32[]{:S(2)}, u32[]{:S(2)}) collective-permute-start(f32[100,128]{1,0:T(8,128)S(1)} %get-tuple-element.24), channel_id=1, source_target_pairs={{224,256},{480,0},{225,257},{481,1},{226,258},{482,2},{227,259},{4... | collective-permute-start | bytes 153608 | tf_op jit(solution)/shard_map/ppermute | solution.py:370
  60.3 9.3 %collective-permute-start.9 = (f32[96,128]{1,0:T(8,128)S(1)}, f32[96,128]{1,0:T(8,128)S(1)}, u32[]{:S(2)}, u32[]{:S(2)}) collective-permute-start(f32[96,128]{1,0:T(8,128)S(1)} %step.8), channel_id=1, source_target_pairs={{0,32},{64,96},{96,128},{128,160},{160,192},{192,224},{256,288},{3... | collective-permute-start | bytes 147464 | tf_op jit(solution)/shard_map/ppermute | solution.py:381
  63.9 13.2 %collective-permute-start.13 = (f32[108,128]{1,0:T(8,128)S(1)}, f32[108,128]{1,0:T(8,128)S(1)}, u32[]{:S(2)}, u32[]{:S(2)}) collective-permute-start(f32[108,128]{1,0:T(8,128)S(1)} %step.7.refs_3_), channel_id=1, source_target_pairs={{224,256},{480,0},{225,257},{481,1},{226,258},{482,2},{227,259},{4... | collective-permute-start | bytes 165896 | tf_op jit(solution)/shard_map/ppermute | solution.py:378
  69.7 6.0 %collective-permute-start.11 = (f32[96,128]{1,0:T(8,128)S(1)}, f32[96,128]{1,0:T(8,128)S(1)}, u32[]{:S(2)}, u32[]{:S(2)}) collective-permute-start(f32[96,128]{1,0:T(8,128)S(1)} %step.10), channel_id=1, source_target_pairs={{0,32},{32,64},{96,128},{128,160},{160,192},{192,224},{256,288},{2... | collective-permute-start | bytes 147464 | tf_op jit(solution)/shard_map/ppermute | solution.py:381
  71.0 7.4 %collective-permute-start.15 = (f32[108,128]{1,0:T(8,128)S(1)}, f32[108,128]{1,0:T(8,128)S(1)}, u32[]{:S(2)}, u32[]{:S(2)}) collective-permute-start(f32[108,128]{1,0:T(8,128)S(1)} %step.9.refs_4_), channel_id=1, source_target_pairs={{224,256},{480,0},{225,257},{481,1},{226,258},{482,2},{227,259},{4... | collective-permute-start | bytes 165896 | tf_op jit(solution)/shard_map/ppermute | solution.py:378
  75.8 8.0 %collective-permute-start.12 = (f32[204,128]{1,0:T(8,128)S(1)}, f32[204,128]{1,0:T(8,128)S(1)}, u32[]{:S(2)}, u32[]{:S(2)}) collective-permute-start(f32[204,128]{1,0:T(8,128)S(1)} %step.11.refs_4_), channel_id=1, source_target_pairs={{224,256},{480,0},{225,257},{481,1},{226,258},{482,2},{227,259},{4... | collective-permute-start | bytes 313352 | tf_op jit(solution)/shard_map/ppermute | solution.py:378
  77.1 6.0 %collective-permute-start.14 = (f32[96,128]{1,0:T(8,128)S(1)}, f32[96,128]{1,0:T(8,128)S(1)}, u32[]{:S(2)}, u32[]{:S(2)}) collective-permute-start(f32[96,128]{1,0:T(8,128)S(1)} %step.12), channel_id=1, source_target_pairs={{0,32},{32,64},{64,96},{128,160},{160,192},{192,224},{256,288},{28... | collective-permute-start | bytes 147464 | tf_op jit(solution)/shard_map/ppermute | solution.py:381
  83.1 0.7 collective-permute-start.16

commit v3 on v2

--- a/solution.py
+++ b/solution.py
@@ -100,8 +100,8 @@
                 values = ref[block, plane * ROWS : (plane + 1) * ROWS, :]
                 high = values.astype(jnp.bfloat16)
                 low = (values - high.astype(jnp.float32)).astype(jnp.bfloat16)
-                table_ref[plane, place * ROWS : (place + 1) * ROWS, :PATCHES] = high
-                table_ref[plane, place * ROWS : (place + 1) * ROWS, PATCHES:] = low
+                table_ref[plane, place * 2 * ROWS : place * 2 * ROWS + ROWS, :] = high
+                table_ref[plane, place * 2 * ROWS + ROWS : (place + 1) * 2 * ROWS, :] = low
             place += 1
 
 
@@ -114,15 +114,15 @@
             rel = rel_ref[row : row + 1, lanes]
             onehot = lax.broadcasted_iota(jnp.int32, (PATCHES, CHUNK), 0) == patch
             onehot = jnp.where(onehot, 1.0, 0.0).astype(jnp.bfloat16)
-            onehot = jnp.concatenate([onehot, onehot], axis=0)
-            found = jnp.dot(table_ref[plane, : len(tiles) * ROWS], onehot, preferred_element_type=jnp.float32)
+            found = jnp.dot(table_ref[plane, : len(tiles) * 2 * ROWS], onehot, preferred_element_type=jnp.float32)
             total = [jnp.zeros((8, CHUNK), jnp.float32) for _ in range(ROWS // 8)]
             wide = jnp.broadcast_to(rel, (8, CHUNK))
             for place, tile in enumerate(tiles):
                 here = wide == tile
                 for part in range(ROWS // 8):
-                    first = place * ROWS + part * 8
-                    total[part] = total[part] + jnp.where(here, found[first : first + 8], 0.0)
+                    first = place * 2 * ROWS + part * 8
+                    both = found[first : first + 8] + found[first + ROWS : first + ROWS + 8]
+                    total[part] = total[part] + jnp.where(here, both, 0.0)
             for part in range(ROWS // 8):
                 for half in range(CHUNK // 128):
                     group = chunk * (CHUNK // 128) + half
@@ -140,7 +140,7 @@
     count = sum(source.shape[0] for source in sources)
     return pl.pallas_call(
         table_kernel,
-        out_shape=jax.ShapeDtypeStruct((2, count * ROWS, 2 * PATCHES), jnp.bfloat16),
+        out_shape=jax.ShapeDtypeStruct((2, count * 2 * ROWS, PATCHES), jnp.bfloat16),
         in_specs=[VMEM] * len(sources),
         out_specs=VMEM,
         compiler_params=LARGE,
@@ -164,13 +164,12 @@
 FOUND = jax.ShapeDtypeStruct((2 * ROWS * GROUPS, 128), jnp.float32)
 
 
-COSTLY = pl.CostEstimate(flops=4000000000, bytes_accessed=100000, transcendentals=0)
-COSTLIER = pl.CostEstimate(flops=16000000000, bytes_accessed=100000, transcendentals=0)
+COSTLY = pl.CostEstimate(flops=16000000000, bytes_accessed=100000, transcendentals=0)
 COST = pl.CostEstimate(flops=100000, bytes_accessed=100000, transcendentals=0)
 
 
 def scratch_table(tiles):
-    return pltpu.VMEM((2, len(tiles) * ROWS, 2 * PATCHES), jnp.bfloat16)
+    return pltpu.VMEM((2, len(tiles) * 2 * ROWS, PATCHES), jnp.bfloat16)
 
 
 def lookup(hops, tiles, sources, rel, patch, before=(), blocks=TILES):
@@ -183,7 +182,7 @@
         input_output_aliases={first + i: i for i in range(len(before))},
         scratch_shapes=[scratch_table(tiles)] if blocks else [],
         compiler_params=LARGE,
-        cost_estimate=COSTLIER if blocks else COST if hops[0] == 1 else COST,
+        cost_estimate=COSTLY if blocks else COST,
         name="lookup",
     )(*sources, rel, patch, *before)
 
@@ -360,18 +359,19 @@
 
     hops = range(HOPS)
     chip = partner("core", 1)
+    mirror = lax.ppermute(join([column], near[:1]), "sky", chip)
     found = lookup(hops, tiles_of((0, 1), 0), [column, near[0]], rel, patch)
-    found = lookup(hops, tiles_of((3,), 0), [near[1]], rel, patch, found)
-    other = [lax.ppermute(join([column, *near], found), "sky", chip), lax.ppermute(far, "sky", chip)]
-    found = list(lookup([0], tiles_of((2,), 0), [far], rel, patch, found[:1])) + list(found[1:])
-    there = tiles_of((0, 1, 3, 2), 1)
-    other = table_of([*other, far])
+    found = lookup(hops, tiles_of((3,), 0) + tiles_of((0,), 1), [near[1], mirror], rel, patch, found)
+    other = lax.ppermute(join([*near, far], found), "sky", chip)
+    found = list(lookup(hops, tiles_of((2,), 0), [far], rel, patch, found))
+    there = tiles_of((1, 3, 2), 1)
+    other = table_of([other])
     moved, leaving = first_step(there, other, rel, patch, rays, found[:1])
     wraps, kept = [lax.ppermute(leaving, "los", across)], moved
     main, before = lax.ppermute(moved, "los", onward(0)), None
     for step in range(1, HOPS + 1):
         if step < HOPS:
-            (found[step],) = lookup([step], there + tiles_of((2,), 0), [other], rel, patch, found[step : step + 1], 0)
+            (found[step],) = lookup([step], there, [other], rel, patch, found[step : step + 1], 0)
         after = ()
         if step < HOPS:
             leaving = run_step(True, step, q, main, None, found)

time: 86.1 us -> 86 us (level)
  the two profiles are of different devices: /device:TPU:56 before, /device:TPU:30 now
where the time goes in v3:
time: 86 us; the launch traced here: 85.3 us
  starting transfers between devices  47 us (55%)
  Pallas kernels  18.1 us (21%)
  waiting for transfers between devices  16.6 us (19%)
  local copies, waits for them, and re-layouts  2.31 us (3%)
  other arithmetic  0.88 us (1%)
    pallas_call x6, Pallas kernels, lookup(): pl.pallas_call(functools.partial(lookup_kernel, hops, tiles, len(sources)...  14.9 us
    ppermute x4, starting transfers between devices, body(): main, before = (lax.ppermute(moved, 'los', onward(step)), main)  13 us
    ppermute x3, starting transfers between devices, body(): lax.ppermute(own, 'sky', partner('z', m))  12.3 us
    ppermute x4, waiting for transfers between devices, body(): main, before = (lax.ppermute(moved, 'los', onward(step)), main)  8.64 us
    ppermute x1, starting transfers between devices, body(): main, before = (lax.ppermute(moved, 'los', onward(0)), None)  4.71 us
    ppermute x1, starting transfers between devices, body(): far = lax.ppermute(column, 'sky', partner('x', 2))  4.03 us
    ppermute x1, waiting for transfers between devices, body(): lax.ppermute(column, 'sky', mixed(1, 3))  4 us
    ppermute x3, waiting for transfers between devices, body(): lax.ppermute(own, 'sky', partner('z', m))  3.92 us
  transfers between devices with their start and end apart: 17, of which 5 were waited for; matrix products, arithmetic and copies ran while one was open for 3% of the time, Pallas kernels for 18%

profile of v3, /device:TPU:30, one launch (start us, length us, event | category | flops | bytes accessed | tf_op | source)
XLA Modules:
  0.0 85.3 jit_solution(10895985244294804723)
XLA Ops:
  0.0 1.2 %coefficients.1 = f32[96,256]{1,0:T(8,128)S(1)} custom-call(bf16[1,2,64,256]{3,2,1,0:T(8,128)(2,1)} %defl_hbm.1, bf16[1,2,96,256]{3,2,1,0:T(8,128)(2,1)} %shear_hbm.1), custom_call_target="tpu_custom_call" | custom-call | tf_op jit(solution)/shard_map/coefficients/pallas_call | solution.py:60
  1.2 4.3 %collective-permute-start = (f32[96,256]{1,0:T(8,128)S(1)}, f32[96,256]{1,0:T(8,128)S(1)}, u32[]{:S(2)}, u32[]{:S(2)}) collective-permute-start(f32[96,256]{1,0:T(8,128)S(1)} %coefficients.1), channel_id=1, source_target_pairs={{0,2},{1,3},{2,0},{3,1},{4,6},{5,7},{6,4},{7,5},{8,10},{9,11},{10,... | collective-permute-start | bytes 294920 | tf_op jit(solution)/shard_map/ppermute | solution.py:355
  5.5 6.1 %collective-permute-start.1 = (f32[96,256]{1,0:T(8,128)S(1)}, f32[96,256]{1,0:T(8,128)S(1)}, u32[]{:S(2)}, u32[]{:S(2)}) collective-permute-start(f32[96,256]{1,0:T(8,128)S(1)} %coefficients.1), channel_id=1, source_target_pairs={{0,4},{1,5},{2,6},{3,7},{4,0},{5,1},{6,2},{7,3},{8,12},{9,13},{10,... | collective-permute-start | bytes 294920 | tf_op jit(solution)/shard_map/ppermute | solution.py:355
  11.6 1.9 %collective-permute-start.2 = (f32[96,256]{1,0:T(8,128)S(1)}, f32[96,256]{1,0:T(8,128)S(1)}, u32[]{:S(2)}, u32[]{:S(2)}) collective-permute-start(f32[96,256]{1,0:T(8,128)S(1)} %coefficients.1), channel_id=1, source_target_pairs={{0,6},{1,7},{2,4},{3,5},{4,2},{5,3},{6,0},{7,1},{8,14},{9,15},{10,... | collective-permute-start | bytes 294920 | tf_op jit(solution)/shard_map/ppermute | solution.py:355
  13.5 0.9 %reduce = s32[4,2,1024]{2,1,0:T(2,128)S(1)} reduce(s32[4,2,1024,1]{2,3,1,0:T(1,128)} %param.8, s32[]{:T(128)} %constant.23.clone.1), dimensions={3}, to_apply=%param.8.reduce_sub_computation | reduce | bytes 65540 | tf_op args[3]
  14.4 0.8 reshape.17.refs_5_.refs_3_.refs_2_.patch_ref
  15.2 0.9 %reshape.18.refs_6_.state_ref = f32[96,128]{1,0:T(8,128)S(1)} reshape(f32[12,1024]{1,0:T(8,128)} %param.5) | data formatting | bytes 98304 | tf_op jit(solution)/shard_map/reshape | solution.py:352
  16.2 3.8 %collective-permute-done.2 = f32[96,256]{1,0:T(8,128)S(1)} collective-permute-done((f32[96,256]{1,0:T(8,128)S(1)}, f32[96,256]{1,0:T(8,128)S(1)}, u32[]{:S(2)}, u32[]{:S(2)}) %collective-permute-start.2) | collective-permute-done | bytes 98336 | tf_op jit(solution)/shard_map/ppermute | solution.py:355
  20.0 2.7 %collective-permute-start.3 = (f32[4,96,256]{2,1,0:T(8,128)S(1)}, f32[4,96,256]{2,1,0:T(8,128)S(1)}, u32[]{:S(2)}, u32[]{:S(2)}) collective-permute-start(f32[4,96,256]{2,1,0:T(8,128)S(1)} %join.3.refs_0_), channel_id=1, source_target_pairs={{0,8},{1,25},{2,10},{3,27},{4,12},{5,29},{6,14},{7,31},{8,0},{9,17... | collective-permute-start | bytes 1179656 | tf_op jit(solution)/shard_map/ppermute | solution.py:357
  22.8 3.0 %collective-permute-start.4 = (f32[4,96,256]{2,1,0:T(8,128)S(1)}, f32[4,96,256]{2,1,0:T(8,128)S(1)}, u32[]{:S(2)}, u32[]{:S(2)}) collective-permute-start(f32[4,96,256]{2,1,0:T(8,128)S(1)} %join.3.refs_0_), channel_id=1, source_target_pairs={{0,24},{1,9},{2,26},{3,11},{4,28},{5,13},{6,30},{7,15},{8,16},{9,1... | collective-permute-start | bytes 1179656 | tf_op jit(solution)/shard_map/ppermute | solution.py:357
  25.8 4.0 %collective-permute-start.5 = (f32[4,96,256]{2,1,0:T(8,128)S(1)}, f32[4,96,256]{2,1,0:T(8,128)S(1)}, u32[]{:S(2)}, u32[]{:S(2)}) collective-permute-start(f32[4,96,256]{2,1,0:T(8,128)S(1)} %join.3.refs_0_), channel_id=1, source_target_pairs={{0,16},{1,17},{2,18},{3,19},{4,20},{5,21},{6,22},{7,23},{8,24},{9,... | collective-permute-start | bytes 1179656 | tf_op jit(solution)/shard_map/ppermute | solution.py:358
  29.9 4.0 %collective-permute-done.3.refs_1_.refs_0_ = f32[4,96,256]{2,1,0:T(8,128)S(1)} collective-permute-done((f32[4,96,256]{2,1,0:T(8,128)S(1)}, f32[4,96,256]{2,1,0:T(8,128)S(1)}, u32[]{:S(2)}, u32[]{:S(2)}) %collective-permute-start.3) | collective-permute-done | bytes 393248 | tf_op jit(solution)/shard_map/ppermute | solution.py:357
  33.9 1.9 %collective-permute-start.6 = (f32[4,96,256]{2,1,0:T(8,128)S(1)}, f32[4,96,256]{2,1,0:T(8,128)S(1)}, u32[]{:S(2)}, u32[]{:S(2)}) collective-permute-start(f32[4,96,256]{2,1,0:T(8,128)S(1)} %join.4), channel_id=1, source_target_pairs={{0,1},{1,0},{2,3},{3,2},{4,5},{5,4},{6,7},{7,6},{8,9},{9,8},{10,11... | collective-permute-start | bytes 1179656 | tf_op jit(solution)/shard_map/ppermute | solution.py:362
  35.8 3.7 %lookup.6 = (f32[768,128]{1,0:T(8,128)S(1)}, f32[768,128]{1,0:T(8,128)S(1)}, f32[768,128]{1,0:T(8,128)S(1)}, f32[768,128]{1,0:T(8,128)S(1)}) custom-call(f32[4,96,256]{2,1,0:T(8,128)S(1)} %join.3.refs_0_, f32[4,96,256]{2,1,0:T(8,128)S(1)} %collective-permute-done.3.refs_1_.refs_0_, s32[8,1024]{1,0:T(8,128)S(1)} %shift-left_xor_fusion.refs_4_.refs_2_.refs_1_.rel_ref, ...), custom_call_target="tpu_custom_call" | custom-call | flops 16000000000 | bytes 100000 | tf_op jit(solution)/shard_map/lookup/pallas_call | solution.py:177
  39.5 4.2 %lookup.7 = (f32[768,128]{1,0:T(8,128)S(1)}, f32[768,128]{1,0:T(8,128)S(1)}, f32[768,128]{1,0:T(8,128)S(1)}, f32[768,128]{1,0:T(8,128)S(1)}) custom-call(f32[4,96,256]{2,1,0:T(8,128)S(1)} %collective-permute-done.4.refs_0_.refs_1_, ...), custom_call_target="tpu_custom_call", output_to_operand_aliasing={{0}: (4, {}), {1}: (5, {}), {2}: (6, {}), {3}: (7, {})} | custom-call | flops 16000000000 | bytes 100000 | tf_op jit(solution)/shard_map/lookup/pallas_call | solution.py:177
  43.9 2.4 %collective-permute-start.7 = (f32[12,96,256]{2,1,0:T(8,128)S(1)}, f32[12,96,256]{2,1,0:T(8,128)S(1)}, u32[]{:S(2)}, u32[]{:S(2)}) collective-permute-start(f32[12,96,256]{2,1,0:T(8,128)S(1)} %join.5), channel_id=1, source_target_pairs={{0,1},{1,0},{2,3},{3,2},{4,5},{5,4},{6,7},{7,6},{8,9},{9,8},{10,11... | collective-permute-start | bytes 3538952 | tf_op jit(solution)/shard_map/ppermute | solution.py:365
  46.3 2.4 %lookup.8 = (f32[768,128]{1,0:T(8,128)S(1)}, f32[768,128]{1,0:T(8,128)S(1)}, f32[768,128]{1,0:T(8,128)S(1)}, f32[768,128]{1,0:T(8,128)S(1)}) custom-call(f32[4,96,256]{2,1,0:T(8,128)S(1)} %collective-permute-done.5.refs_2_.refs_0_, ...), custom_call_target="tpu_custom_call", output_to_operand_aliasing={{0}: (3, {}), {1}: (4, {}), {2}: (5, {}), {3}: (6, {})} | custom-call | flops 16000000000 | bytes 100000 | tf_op jit(solution)/shard_map/lookup/pallas_call | solution.py:177
  48.9 1.4 %first_step.1 = (f32[96,128]{1,0:T(8,128)S(1)}, f32[100,128]{1,0:T(8,128)S(1)}) custom-call(bf16[2,1152,256]{2,1,0:T(8,128)(2,1)S(1)} %table.1.table_ref.refs_0_, s32[8,1024]{1,0:T(8,128)S(1)} %shift-left_xor_fusion.refs_4_.refs_2_.refs_1_.rel_ref, s32[8,1024]{1,0:T(8,128)S(1)} %reshape.17.refs_5_.refs_3_.refs_2_.patch_ref, ...), custom_call_target="tpu_custom_call" | custom-call | flops 100000 | bytes 100000 | tf_op jit(solution)/shard_map/first_step/pallas_call | solution.py:266
  50.3 4.7 %collective-permute-start.8 = (f32[96,128]{1,0:T(8,128)S(1)}, f32[96,128]{1,0:T(8,128)S(1)}, u32[]{:S(2)}, u32[]{:S(2)}) collective-permute-start(f32[96,128]{1,0:T(8,128)S(1)} %get-tuple-element.28.refs_1_), channel_id=1, source_target_pairs={{32,64},{64,96},{96,128},{128,160},{160,192},{192,224},{288,320},{... | collective-permute-start | bytes 147464 | tf_op jit(solution)/shard_map/ppermute | solution.py:371
  55.0 0.8 collective-permute-start.10
  55.9 1.5 %lookup.9.refs_1_.refs_2_.refs_3_ = f32[768,128]{1,0:T(8,128)S(1)} custom-call(bf16[2,1152,256]{2,1,0:T(8,128)(2,1)S(1)} %table.1.table_ref.refs_0_, s32[8,1024]{1,0:T(8,128)S(1)} %shift-left_xor_fusion.refs_4_.refs_2_.refs_1_.rel_ref, s32[8,1024]{1,0:T(8,128)S(1)} %reshape.17.refs_5_.refs_3_.refs_2_.patch_ref, ...), custom_call_target="tpu_custom_call", output_to_operand_aliasing={{}: (3, {})} | custom-call | flops 100000 | bytes 100000 | tf_op jit(solution)/shard_map/lookup/pallas_call | solution.py:177
  57.5 4.8 %collective-permute-start.9 = (f32[96,128]{1,0:T(8,128)S(1)}, f32[96,128]{1,0:T(8,128)S(1)}, u32[]{:S(2)}, u32[]{:S(2)}) collective-permute-start(f32[96,128]{1,0:T(8,128)S(1)} %step.8), channel_id=1, source_target_pairs={{0,32},{64,96},{96,128},{128,160},{160,192},{192,224},{256,288},{3... | collective-permute-start | bytes 147464 | tf_op jit(solution)/shard_map/ppermute | solution.py:381
  62.3 1.5 %lookup.10.refs_1_.refs_2_.refs_3_ = f32[768,128]{1,0:T(8,128)S(1)} custom-call(bf16[2,1152,256]{2,1,0:T(8,128)(2,1)S(1)} %table.1.table_ref.refs_0_, s32[8,1024]{1,0:T(8,128)S(1)} %shift-left_xor_fusion.refs_4_.refs_2_.refs_1_.rel_ref, s32[8,1024]{1,0:T(8,128)S(1)} %reshape.17.refs_5_.refs_3_.refs_2_.patch_ref, ...), custom_call_target="tpu_custom_call", output_to_operand_aliasing={{}: (3, {})} | custom-call | flops 100000 | bytes 100000 | tf_op jit(solution)/shard_map/lookup/pallas_call | solution.py:177
  63.8 0.7 collective-permute-start.13
  64.6 4.9 %collective-permute-start.11 = (f32[96,128]{1,0:T(8,128)S(1)}, f32[96,128]{1,0:T(8,128)S(1)}, u32[]{:S(2)}, u32[]{:S(2)}) collective-permute-start(f32[96,128]{1,0:T(8,128)S(1)} %step.10), channel_id=1, source_target_pairs={{0,32},{32,64},{96,128},{128,160},{160,192},{192,224},{256,288},{2... | collective-permute-start | bytes 147464 | tf_op jit(solution)/shard_map/ppermute | solution.py:381
  69.6 0.7 collective-permute-start.15
  70.3 1.5 %lookup.11.refs_1_.refs_2_ = f32[768,128]{1,0:T(8,128)S(1)} custom-call(bf16[2,1152,256]{2,1,0:T(8,128)(2,1)S(1)} %table.1.table_ref.refs_0_, s32[8,1024]{1,0:T(8,128)S(1)} %shift-left_xor_fusion.refs_4_.refs_2_.refs_1_.rel_ref, s32[8,1024]{1,0:T(8,128)S(1)} %reshape.17.refs_5_.refs_3_.refs_2_.patch_ref, ...), custom_call_target="tpu_custom_call", output_to_operand_aliasing={{}: (3, {})} | custom-call | flops 100000 | bytes 100000 | tf_op jit(solution)/shard_map/lookup/pallas_call | solution.py:177
  71.8 0.7 collective-permute-start.12
  72.6 1.3 %collective-permute-start.14 = (f32[96,128]{1,0:T(8,128)S(1)}, f32[96,128]{1,0:T(8,128)S(1)}, u32[]{:S(2)}, u32[]{:S(2)}) collective-permute-start(f32[96,128]{1,0:T(8,128)S(1)} %step.12), channel_id=1, source_target_pairs={{0,32},{32,64},{64,96},{128,160},{160,192},{192,224},{256,288},{28... | collective-permute-start | bytes 147464 | tf_op jit(solution)/shard_map/ppermute | solution.py:381
  73.9 4.7 %collective-permute-done.14.refs_0_ = f32[96,128]{1,0:T(8,128)S(1)} collective-permute-done((f32[96,128]{1,0:T(8,128)S(1)}, f32[96,128]{1,0:T(8,128)S(1)}, u32[]{:S(2)}, u32[]{:S(2)}) %collective-permute-start.14) | collective-permute-done | bytes 49184 | tf_op jit(solution)/shard_map/ppermute | solution.py:381
  78.7 2.0 %collective-permute-start.16 = (f32[96,128]{1,0:T(8,128)S(1)}, f32[96,128]{1,0:T(8,128)S(1)}, u32[]{:S(2)}, u32[]{:S(2)}) collective-permute-start(f32[96,128]{1,0:T(8,128)S(1)} %step.13), channel_id=1, source_target_pairs={{0,32},{32,64},{64,96},{96,128},{256,288},{288,320},{320,352},{352... | collective-permute-start | bytes 147464 | tf_op jit(solution)/shard_map/ppermute | solution.py:381
  80.7 4.0 %collective-permute-done.16 = f32[96,128]{1,0:T(8,128)S(1)} collective-permute-done((f32[96,128]{1,0:T(8,128)S(1)}, f32[96,128]{1,0:T(8,128)S(1)}, u32[]{:S(2)}, u32[]{:S(2)}) %collective-permute-start.16) | collective-permute-done | bytes 49184 | tf_op jit(solution)/shard_map/ppermute | solution.py:381
  (28 shorter events, 1.5 us)
Async XLA Ops:
  1.2 14.9 %collective-permute-start = (f32[96,256]{1,0:T(8,128)S(1)}, f32[96,256]{1,0:T(8,128)S(1)}, u32[]{:S(2)}, u32[]{:S(2)}) collective-permute-start(f32[96,256]{1,0:T(8,128)S(1)} %coefficients.1), channel_id=1, source_target_pairs={{0,2},{1,3},{2,0},{3,1},{4,6},{5,7},{6,4},{7,5},{8,10},{9,11},{10,... | collective-permute-start | bytes 294920 | tf_op jit(solution)/shard_map/ppermute | solution.py:355
  5.5 10.7 %collective-permute-start.1 = (f32[96,256]{1,0:T(8,128)S(1)}, f32[96,256]{1,0:T(8,128)S(1)}, u32[]{:S(2)}, u32[]{:S(2)}) collective-permute-start(f32[96,256]{1,0:T(8,128)S(1)} %coefficients.1), channel_id=1, source_target_pairs={{0,4},{1,5},{2,6},{3,7},{4,0},{5,1},{6,2},{7,3},{8,12},{9,13},{10,... | collective-permute-start | bytes 294920 | tf_op jit(solution)/shard_map/ppermute | solution.py:355
  11.6 8.4 %collective-permute-start.2 = (f32[96,256]{1,0:T(8,128)S(1)}, f32[96,256]{1,0:T(8,128)S(1)}, u32[]{:S(2)}, u32[]{:S(2)}) collective-permute-start(f32[96,256]{1,0:T(8,128)S(1)} %coefficients.1), channel_id=1, source_target_pairs={{0,6},{1,7},{2,4},{3,5},{4,2},{5,3},{6,0},{7,1},{8,14},{9,15},{10,... | collective-permute-start | bytes 294920 | tf_op jit(solution)/shard_map/ppermute | solution.py:355
  20.0 13.8 %collective-permute-start.3 = (f32[4,96,256]{2,1,0:T(8,128)S(1)}, f32[4,96,256]{2,1,0:T(8,128)S(1)}, u32[]{:S(2)}, u32[]{:S(2)}) collective-permute-start(f32[4,96,256]{2,1,0:T(8,128)S(1)} %join.3.refs_0_), channel_id=1, source_target_pairs={{0,8},{1,25},{2,10},{3,27},{4,12},{5,29},{6,14},{7,31},{8,0},{9,17... | collective-permute-start | bytes 1179656 | tf_op jit(solution)/shard_map/ppermute | solution.py:357
  22.8 16.8 %collective-permute-start.4 = (f32[4,96,256]{2,1,0:T(8,128)S(1)}, f32[4,96,256]{2,1,0:T(8,128)S(1)}, u32[]{:S(2)}, u32[]{:S(2)}) collective-permute-start(f32[4,96,256]{2,1,0:T(8,128)S(1)} %join.3.refs_0_), channel_id=1, source_target_pairs={{0,24},{1,9},{2,26},{3,11},{4,28},{5,13},{6,30},{7,15},{8,16},{9,1... | collective-permute-start | bytes 1179656 | tf_op jit(solution)/shard_map/ppermute | solution.py:357
  25.8 17.9 %collective-permute-start.5 = (f32[4,96,256]{2,1,0:T(8,128)S(1)}, f32[4,96,256]{2,1,0:T(8,128)S(1)}, u32[]{:S(2)}, u32[]{:S(2)}) collective-permute-start(f32[4,96,256]{2,1,0:T(8,128)S(1)} %join.3.refs_0_), channel_id=1, source_target_pairs={{0,16},{1,17},{2,18},{3,19},{4,20},{5,21},{6,22},{7,23},{8,24},{9,... | collective-permute-start | bytes 1179656 | tf_op jit(solution)/shard_map/ppermute | solution.py:358
  33.9 5.6 %collective-permute-start.6 = (f32[4,96,256]{2,1,0:T(8,128)S(1)}, f32[4,96,256]{2,1,0:T(8,128)S(1)}, u32[]{:S(2)}, u32[]{:S(2)}) collective-permute-start(f32[4,96,256]{2,1,0:T(8,128)S(1)} %join.4), channel_id=1, source_target_pairs={{0,1},{1,0},{2,3},{3,2},{4,5},{5,4},{6,7},{7,6},{8,9},{9,8},{10,11... | collective-permute-start | bytes 1179656 | tf_op jit(solution)/shard_map/ppermute | solution.py:362
  43.9 4.9 %collective-permute-start.7 = (f32[12,96,256]{2,1,0:T(8,128)S(1)}, f32[12,96,256]{2,1,0:T(8,128)S(1)}, u32[]{:S(2)}, u32[]{:S(2)}) collective-permute-start(f32[12,96,256]{2,1,0:T(8,128)S(1)} %join.5), channel_id=1, source_target_pairs={{0,1},{1,0},{2,3},{3,2},{4,5},{5,4},{6,7},{7,6},{8,9},{9,8},{10,11... | collective-permute-start | bytes 3538952 | tf_op jit(solution)/shard_map/ppermute | solution.py:365
  50.3 7.1 %collective-permute-start.8 = (f32[96,128]{1,0:T(8,128)S(1)}, f32[96,128]{1,0:T(8,128)S(1)}, u32[]{:S(2)}, u32[]{:S(2)}) collective-permute-start(f32[96,128]{1,0:T(8,128)S(1)} %get-tuple-element.28.refs_1_), channel_id=1, source_target_pairs={{32,64},{64,96},{96,128},{128,160},{160,192},{192,224},{288,320},{... | collective-permute-start | bytes 147464 | tf_op jit(solution)/shard_map/ppermute | solution.py:371
  55.0 9.5 %collective-permute-start.10 = (f32[100,128]{1,0:T(8,128)S(1)}, f32[100,128]{1,0:T(8,128)S(1)}, u32[]{:S(2)}, u32[]{:S(2)}) collective-permute-start(f32[100,128]{1,0:T(8,128)S(1)} %get-tuple-element.30), channel_id=1, source_target_pairs={{224,256},{480,0},{225,257},{481,1},{226,258},{482,2},{227,259},{4... | collective-permute-start | bytes 153608 | tf_op jit(solution)/shard_map/ppermute | solution.py:370
  57.5 7.0 %collective-permute-start.9 = (f32[96,128]{1,0:T(8,128)S(1)}, f32[96,128]{1,0:T(8,128)S(1)}, u32[]{:S(2)}, u32[]{:S(2)}) collective-permute-start(f32[96,128]{1,0:T(8,128)S(1)} %step.8), channel_id=1, source_target_pairs={{0,32},{64,96},{96,128},{128,160},{160,192},{192,224},{256,288},{3... | collective-permute-start | bytes 147464 | tf_op jit(solution)/shard_map/ppermute | solution.py:381
  63.8 8.7 %collective-permute-start.13 = (f32[108,128]{1,0:T(8,128)S(1)}, f32[108,128]{1,0:T(8,128)S(1)}, u32[]{:S(2)}, u32[]{:S(2)}) collective-permute-start(f32[108,128]{1,0:T(8,128)S(1)} %step.7.refs_3_), channel_id=1, source_target_pairs={{224,256},{480,0},{225,257},{481,1},{226,258},{482,2},{227,259},{4... | collective-permute-start | bytes 165896 | tf_op jit(solution)/shard_map/ppermute | solution.py:378
  64.6 7.2 %collective-permute-start.11 = (f32[96,128]{1,0:T(8,128)S(1)}, f32[96,128]{1,0:T(8,128)S(1)}, u32[]{:S(2)}, u32[]{:S(2)}) collective-permute-start(f32[96,128]{1,0:T(8,128)S(1)} %step.10), channel_id=1, source_target_pairs={{0,32},{32,64},{96,128},{128,160},{160,192},{192,224},{256,288},{2... | collective-permute-start | bytes 147464 | tf_op jit(solution)/shard_map/ppermute | solution.py:381
  69.6 4.3 %collective-permute-start.15 = (f32[108,128]{1,0:T(8,128)S(1)}, f32[108,128]{1,0:T(8,128)S(1)}, u32[]{:S(2)}, u32[]{:S(2)}) collective-permute-start(f32[108,128]{1,0:T(8,128)S(1)} %step.9.refs_4_), channel_id=1, source_target_pairs={{224,256},{480,0},{225,257},{481,1},{226,258},{482,2},{227,259},{4... | collective-permute-start | bytes 165896 | tf_op jit(solution)/shard_map/ppermute | solution.py:378
  71.8 12.8 %collective-permute-start.12 = (f32[204,128]{1,0:T(8,128)S(1)}, f32[204,128]{1,0:T(8,128)S(1)}, u32[]{:S(2)}, u32[]{:S(2)}) collective-permute-start(f32[204,128]{1,0:T(8,128)S(1)} %step.11.refs_4_), channel_id=1, source_target_pairs={{224,256},{480,0},{225,257},{481,1},{226,258},{482,2},{227,259},{4... | collective-permute-start | bytes 313352 | tf_op jit(solution)/shard_map/ppermute | solution.py:378
  72.6 6.0 %collective-permute-start.14 = (f32[96,128]{1,0:T(8,128)S(1)}, f32[96,128]{1,0:T(8,128)S(1)}, u32[]{:S(2)}, u32[]{:S(2)}) collective-permute-start(f32[96,128]{1,0:T(8,128)S(1)} %step.12), channel_id=1, source_target_pairs={{0,32},{32,64},{64,96},{128,160},{160,192},{192,224},{256,288},{28... | collective-permute-start | bytes 147464 | tf_op jit(solution)/shard_map/ppermute | solution.py:381
  78.7 6.0 %collective-permute-start.16 = (f32[96,128]{1,0:T(8,128)S(1)}, f32[96,128]{1,0:T(8,128)S(1)}, u32[]{:S(2)}, u32[]{:S(2)}) collective-permute-start(f32[96,128]{1,0:T(8,128)S(1)} %step.13), channel_id=1, source_target_pairs={{0,32},{32,64},{64,96},{96,128},{256,288},{288,320},{320,352},{352... | collective-permute-start | bytes 147464 | tf_op jit(solution)/shard_map/ppermute | solution.py:381
